TPU v7x, 32 devices: a whole 2x2x4 slice. The times are simulated.
32 devices in a mesh: rep: 2 (over x), fsdp: 4 (over z), ctx: 4 (over y, core).
Axes of the slice: x: 2, y: 2, z: 4, core: 2. Of those that a mesh axis runs over, the one named last changes fastest.
Arguments:
- tokens: bfloat16 [8, 1024, 768], P(('rep', 'fsdp'), 'ctx'), may hold values from -2.5 to 2.5
- lengths: int32 [8], P(('rep', 'fsdp')), may hold values from 256 to 1024, as said below
- cotangent: bfloat16 [8, 1024, 768], P(('rep', 'fsdp'), 'ctx'), may hold values from -8 to 8
- w_qkv: bfloat16 [2, 3, 768, 768], P(None, None, 'fsdp'), may hold values from -0.21875 to 0.21875
- w_attn_out: bfloat16 [2, 768, 768], P(None, 'fsdp'), may hold values from -1.1953125 to 1.1953125
- w_in: bfloat16 [2, 768, 3072], P(None, 'fsdp'), may hold values from -0.21875 to 0.21875
- w_out: bfloat16 [2, 3072, 768], P(None, 'fsdp'), may hold values from -0.109375 to 0.109375
- bias_q: bfloat16 [2, 768], P(None, 'fsdp'), may hold values from -0.75 to 0.75
- bias_d: bfloat16 [2, 3, 768], P(None, None, 'fsdp'), may hold values from -0.25 to 0.25
- bias_ff: bfloat16 [2, 3072], P(None, 'fsdp'), may hold values from -0.75 to 0.75
- norm_gain: bfloat16 [2, 2, 768], P(None, None, 'fsdp'), may hold values from 0.5 to 1.5
- norm_shift: bfloat16 [2, 2, 768], P(None, None, 'fsdp'), may hold values from -0.75 to 0.75
Outputs:
- output_tokens: bfloat16 [8, 1024, 768], P(('rep', 'fsdp'), 'ctx')
- grad_tokens: float32 [8, 1024, 768], P(('rep', 'fsdp'), 'ctx')
- grad_w_qkv: float32 [2, 3, 768, 768], P(None, None, 'fsdp')
- grad_w_attn_out: float32 [2, 768, 768], P(None, 'fsdp')
- grad_w_in: float32 [2, 768, 3072], P(None, 'fsdp')
- grad_w_out: float32 [2, 3072, 768], P(None, 'fsdp')
- grad_bias_q: float32 [2, 768], P(None, 'fsdp')
- grad_bias_d: float32 [2, 3, 768], P(None, None, 'fsdp')
- grad_bias_ff: float32 [2, 3072], P(None, 'fsdp')
- grad_norm_gain: float32 [2, 2, 768], P(None, None, 'fsdp')
- grad_norm_shift: float32 [2, 2, 768], P(None, None, 'fsdp')
Inputs may be any that keep to these rules, and one draw needn't show every extreme that they name: `lengths`: some sequence has exactly 1024 valid tokens and some other exactly 256.
All inputs are finite; a program needn't handle non-finite values.
Results may differ from a plain program's by a relative error of at most 0.02.
Values may be sent and summed in bfloat16 or wider, within the bound.
A program may use at most 256 MiB of HBM per device.

v0:
```python
import jax
import jax.numpy as jnp
from jax import lax
from jax.sharding import PartitionSpec as P

HEADS = 12
HEAD = 64


epsilon = 1e-05
score_scale = 0.125
masked_value = -1e30


def layer_norm(operand, scale_row, shift_row):
    center = operand - jnp.mean(operand, axis=-1, keepdims=True)
    variance = jnp.mean(center * center, axis=-1, keepdims=True)
    return center * lax.rsqrt(variance + epsilon) * scale_row + shift_row


def matmul(operand_a, operand_b):
    return jnp.dot(operand_a, operand_b, preferred_element_type=jnp.float32)


def matmul_left_t(operand_a, operand_b):
    return lax.dot_general(
        operand_a, operand_b, (((0,), (0,)), ((), ())), preferred_element_type=jnp.float32
    )


def matmul_right_t(operand_a, operand_b):
    return lax.dot_general(
        operand_a, operand_b, (((1,), (1,)), ((), ())), preferred_element_type=jnp.float32
    )


def head_slices(matrix, group_idx, row_count):
    piece_cols = lax.dynamic_slice_in_dim(matrix, group_idx * (2 * HEAD), 2 * HEAD, 1)
    return piece_cols.reshape(row_count, 2, HEAD)


def group_scores(query_part, key_part, key_ok):
    scores = (
        jnp.einsum("qhd,khd->hqk", query_part, key_part, preferred_element_type=jnp.float32)
        * score_scale
    )
    return jnp.where(key_ok[None, None, :], scores, masked_value)


def attend_forward(queries, key_all, value_all, key_ok):
    row_count = queries.shape[0]
    key_count = key_all.shape[0]

    def per_group(group_idx):
        query_part = head_slices(queries, group_idx, row_count)
        key_part = head_slices(key_all, group_idx, key_count)
        value_part = head_slices(value_all, group_idx, key_count)
        scores = group_scores(query_part, key_part, key_ok)
        peak = jnp.max(scores, axis=-1, keepdims=True)
        shifted_exp = jnp.exp(scores - peak)
        summed = jnp.sum(shifted_exp, axis=-1, keepdims=True)
        probs = (shifted_exp / summed).astype(jnp.bfloat16)
        mixed = jnp.einsum("hqk,khd->qhd", probs, value_part, preferred_element_type=jnp.float32)
        log_sum = peak[..., 0] + jnp.log(summed[..., 0])
        return (mixed.reshape(row_count, 2 * HEAD), log_sum)

    mixed, log_sum = lax.map(per_group, jnp.arange(HEADS // 2))
    return (mixed.transpose(1, 0, 2).reshape(row_count, HEADS * HEAD), log_sum)


def attend_backward(queries, key_all, value_all, key_ok, grad_mixed, log_sum):
    row_count = queries.shape[0]
    key_count = key_all.shape[0]

    def per_group(items):
        group_idx, group_lse = items
        query_part = head_slices(queries, group_idx, row_count)
        key_part = head_slices(key_all, group_idx, key_count)
        value_part = head_slices(value_all, group_idx, key_count)
        grad_part = head_slices(grad_mixed, group_idx, row_count)
        scores = group_scores(query_part, key_part, key_ok)
        probs = jnp.exp(scores - group_lse[..., None])
        grad_probs = jnp.einsum(
            "qhd,khd->hqk", grad_part, value_part, preferred_element_type=jnp.float32
        )
        inner = jnp.sum(probs * grad_probs, axis=-1, keepdims=True)
        grad_scores = (probs * (grad_probs - inner)).astype(jnp.bfloat16)
        grad_query = (
            jnp.einsum("hqk,khd->qhd", grad_scores, key_part, preferred_element_type=jnp.float32)
            * score_scale
        )
        grad_key = (
            jnp.einsum("hqk,qhd->khd", grad_scores, query_part, preferred_element_type=jnp.float32)
            * score_scale
        )
        grad_value = jnp.einsum(
            "hqk,qhd->khd",
            probs.astype(jnp.bfloat16),
            grad_part,
            preferred_element_type=jnp.float32,
        )
        return (
            grad_query.reshape(row_count, 2 * HEAD),
            grad_key.reshape(key_count, 2 * HEAD),
            grad_value.reshape(key_count, 2 * HEAD),
        )

    grad_query, grad_key, grad_value = lax.map(per_group, (jnp.arange(HEADS // 2), log_sum))
    grad_query = grad_query.transpose(1, 0, 2).reshape(row_count, HEADS * HEAD)
    grad_key = grad_key.transpose(1, 0, 2).reshape(key_count, HEADS * HEAD)
    grad_value = grad_value.transpose(1, 0, 2).reshape(key_count, HEADS * HEAD)
    return (grad_query, grad_key, grad_value)


def block_forward(inputs, weights_full, length):
    qkv_mats, out_mat, in_mat, down_mat, query_bias, bias_rows, ffn_bias, gains, shifts = (
        weights_full
    )
    gains_f = gains.astype(jnp.float32)
    shifts_f = shifts.astype(jnp.float32)
    rounded = inputs.astype(jnp.bfloat16)
    queries = (matmul(rounded, qkv_mats[0]) + query_bias.astype(jnp.float32)).astype(jnp.bfloat16)
    key_rows = matmul(rounded, qkv_mats[1]).astype(jnp.bfloat16)
    value_rows = (matmul(rounded, qkv_mats[2]) + bias_rows[0].astype(jnp.float32)).astype(
        jnp.bfloat16
    )
    key_all, value_all = (
        lax.all_gather(key_rows, "ctx", axis=0, tiled=True),
        lax.all_gather(value_rows, "ctx", axis=0, tiled=True),
    )
    key_ok = jnp.arange(key_all.shape[0]) < length
    mixed_sum, log_sum = attend_forward(queries, key_all, value_all, key_ok)
    mixed = mixed_sum.astype(jnp.bfloat16)
    first_sum = inputs + matmul(mixed, out_mat) + bias_rows[1].astype(jnp.float32)
    normed = layer_norm(first_sum, gains_f[0], shifts_f[0])
    hidden = matmul(normed.astype(jnp.bfloat16), in_mat) + ffn_bias.astype(jnp.float32)
    active = jax.nn.gelu(hidden, approximate=False).astype(jnp.bfloat16)
    second_sum = normed + matmul(active, down_mat) + bias_rows[2].astype(jnp.float32)
    output = layer_norm(second_sum, gains_f[1], shifts_f[1])
    kept_acts = (
        rounded,
        queries,
        key_all,
        value_all,
        key_ok,
        mixed,
        log_sum,
        first_sum,
        normed,
        hidden,
        active,
        second_sum,
    )
    return (output, kept_acts)


def block_backward(grad_output, weights_full, kept_acts):
    qkv_mats, out_mat, in_mat, down_mat, query_bias, bias_rows, ffn_bias, gains, shifts = (
        weights_full
    )
    (
        rounded,
        queries,
        key_all,
        value_all,
        key_ok,
        mixed,
        log_sum,
        first_sum,
        normed,
        hidden,
        active,
        second_sum,
    ) = kept_acts
    gains_f = gains.astype(jnp.float32)
    shifts_f = shifts.astype(jnp.float32)
    unused_second, pull_second = jax.vjp(layer_norm, second_sum, gains_f[1], shifts_f[1])
    grad_second, grad_gain_two, grad_shift_two = pull_second(grad_output)
    grad_update = grad_second.astype(jnp.bfloat16)
    grad_down = matmul_left_t(active, grad_update)
    grad_bias_three = jnp.sum(grad_update.astype(jnp.float32), axis=0)
    grad_active = matmul_right_t(grad_update, down_mat)
    unused_gelu, pull_gelu = jax.vjp(
        lambda pre_act: jax.nn.gelu(pre_act, approximate=False), hidden
    )
    grad_hidden = pull_gelu(grad_active)[0].astype(jnp.bfloat16)
    grad_in = matmul_left_t(normed.astype(jnp.bfloat16), grad_hidden)
    grad_ffn_bias = jnp.sum(grad_hidden.astype(jnp.float32), axis=0)
    grad_normed = grad_second + matmul_right_t(grad_hidden, in_mat)
    unused_first, pull_first = jax.vjp(layer_norm, first_sum, gains_f[0], shifts_f[0])
    grad_first, grad_gain_one, grad_shift_one = pull_first(grad_normed)
    grad_branch = grad_first.astype(jnp.bfloat16)
    grad_out_mat = matmul_left_t(mixed, grad_branch)
    grad_bias_two = jnp.sum(grad_branch.astype(jnp.float32), axis=0)
    grad_mixed = matmul_right_t(grad_branch, out_mat).astype(jnp.bfloat16)
    grad_query, grad_key_all, grad_value_all = attend_backward(
        queries, key_all, value_all, key_ok, grad_mixed, log_sum
    )
    grad_key, grad_value = (
        lax.psum_scatter(
            grad_key_all.astype(jnp.bfloat16), "ctx", scatter_dimension=0, tiled=True
        ).astype(jnp.float32),
        lax.psum_scatter(
            grad_value_all.astype(jnp.bfloat16), "ctx", scatter_dimension=0, tiled=True
        ).astype(jnp.float32),
    )
    grad_query = grad_query.astype(jnp.bfloat16)
    grad_key = grad_key.astype(jnp.bfloat16)
    grad_value = grad_value.astype(jnp.bfloat16)
    grad_qkv = jnp.stack(
        [
            matmul_left_t(rounded, grad_query),
            matmul_left_t(rounded, grad_key),
            matmul_left_t(rounded, grad_value),
        ],
        axis=0,
    )
    grad_query_bias = jnp.sum(grad_query.astype(jnp.float32), axis=0)
    grad_bias_value = jnp.sum(grad_value.astype(jnp.float32), axis=0)
    grad_inputs = (
        grad_first
        + matmul_right_t(grad_query, qkv_mats[0])
        + matmul_right_t(grad_key, qkv_mats[1])
        + matmul_right_t(grad_value, qkv_mats[2])
    )
    grads_block = (
        grad_qkv,
        grad_out_mat,
        grad_in,
        grad_down,
        grad_query_bias,
        jnp.stack([grad_bias_value, grad_bias_two, grad_bias_three], axis=0),
        grad_ffn_bias,
        jnp.stack([grad_gain_one, grad_gain_two], axis=0),
        jnp.stack([grad_shift_one, grad_shift_two], axis=0),
    )
    return (grad_inputs, grads_block)


def body(
    tokens,
    lengths,
    cotangent,
    w_qkv,
    w_attn_out,
    w_in,
    w_out,
    bias_q,
    bias_d,
    bias_ff,
    norm_gain,
    norm_shift,
):
    length = lengths[0]
    row_count = tokens.shape[1]
    first_row = lax.axis_index("ctx") * row_count
    valid_rows = (first_row + jnp.arange(row_count) < length).astype(jnp.float32)
    carried = tokens[0].astype(jnp.float32)
    kept_weights = []
    kept_layers = []
    for layer_idx in range(2):
        weights_full = (
            lax.all_gather(w_qkv[layer_idx], "fsdp", axis=1, tiled=True),
            lax.all_gather(w_attn_out[layer_idx], "fsdp", axis=0, tiled=True),
            lax.all_gather(w_in[layer_idx], "fsdp", axis=0, tiled=True),
            lax.all_gather(w_out[layer_idx], "fsdp", axis=0, tiled=True),
            lax.all_gather(bias_q[layer_idx], "fsdp", axis=0, tiled=True),
            lax.all_gather(bias_d[layer_idx], "fsdp", axis=1, tiled=True),
            lax.all_gather(bias_ff[layer_idx], "fsdp", axis=0, tiled=True),
            lax.all_gather(norm_gain[layer_idx], "fsdp", axis=1, tiled=True),
            lax.all_gather(norm_shift[layer_idx], "fsdp", axis=1, tiled=True),
        )
        kept_weights.append(weights_full)
        carried, kept_acts = block_forward(carried, weights_full, length)
        kept_layers.append(kept_acts)
    output_tokens = carried.astype(jnp.bfloat16)[None]
    grad_carried = cotangent[0].astype(jnp.float32) * valid_rows[:, None]
    reduced = [None, None]
    for layer_idx in (1, 0):
        weights_full = (
            lax.all_gather(w_qkv[layer_idx], "fsdp", axis=1, tiled=True),
            lax.all_gather(w_attn_out[layer_idx], "fsdp", axis=0, tiled=True),
            lax.all_gather(w_in[layer_idx], "fsdp", axis=0, tiled=True),
            lax.all_gather(w_out[layer_idx], "fsdp", axis=0, tiled=True),
            lax.all_gather(bias_q[layer_idx], "fsdp", axis=0, tiled=True),
            lax.all_gather(bias_d[layer_idx], "fsdp", axis=1, tiled=True),
            lax.all_gather(bias_ff[layer_idx], "fsdp", axis=0, tiled=True),
            lax.all_gather(norm_gain[layer_idx], "fsdp", axis=1, tiled=True),
            lax.all_gather(norm_shift[layer_idx], "fsdp", axis=1, tiled=True),
        )
        grad_carried, grads_block = block_backward(
            grad_carried, weights_full, kept_layers[layer_idx]
        )
        shard_sums = (
            lax.psum_scatter(
                grads_block[0].astype(jnp.bfloat16), "fsdp", scatter_dimension=1, tiled=True
            ).astype(jnp.float32),
            lax.psum_scatter(
                grads_block[1].astype(jnp.bfloat16), "fsdp", scatter_dimension=0, tiled=True
            ).astype(jnp.float32),
            lax.psum_scatter(
                grads_block[2].astype(jnp.bfloat16), "fsdp", scatter_dimension=0, tiled=True
            ).astype(jnp.float32),
            lax.psum_scatter(
                grads_block[3].astype(jnp.bfloat16), "fsdp", scatter_dimension=0, tiled=True
            ).astype(jnp.float32),
            lax.psum_scatter(
                grads_block[4].astype(jnp.bfloat16), "fsdp", scatter_dimension=0, tiled=True
            ).astype(jnp.float32),
            lax.psum_scatter(
                grads_block[5].astype(jnp.bfloat16), "fsdp", scatter_dimension=1, tiled=True
            ).astype(jnp.float32),
            lax.psum_scatter(
                grads_block[6].astype(jnp.bfloat16), "fsdp", scatter_dimension=0, tiled=True
            ).astype(jnp.float32),
            lax.psum_scatter(
                grads_block[7].astype(jnp.bfloat16), "fsdp", scatter_dimension=1, tiled=True
            ).astype(jnp.float32),
            lax.psum_scatter(
                grads_block[8].astype(jnp.bfloat16), "fsdp", scatter_dimension=1, tiled=True
            ).astype(jnp.float32),
        )
        reduced[layer_idx] = (
            lax.psum(shard_sums[0].astype(jnp.bfloat16), ("rep", "ctx")).astype(jnp.float32),
            lax.psum(shard_sums[1].astype(jnp.bfloat16), ("rep", "ctx")).astype(jnp.float32),
            lax.psum(shard_sums[2].astype(jnp.bfloat16), ("rep", "ctx")).astype(jnp.float32),
            lax.psum(shard_sums[3].astype(jnp.bfloat16), ("rep", "ctx")).astype(jnp.float32),
            lax.psum(shard_sums[4].astype(jnp.bfloat16), ("rep", "ctx")).astype(jnp.float32),
            lax.psum(shard_sums[5].astype(jnp.bfloat16), ("rep", "ctx")).astype(jnp.float32),
            lax.psum(shard_sums[6].astype(jnp.bfloat16), ("rep", "ctx")).astype(jnp.float32),
            lax.psum(shard_sums[7].astype(jnp.bfloat16), ("rep", "ctx")).astype(jnp.float32),
            lax.psum(shard_sums[8].astype(jnp.bfloat16), ("rep", "ctx")).astype(jnp.float32),
        )
    stacked = [jnp.stack([reduced[0][member], reduced[1][member]], axis=0) for member in range(9)]
    return (
        output_tokens,
        grad_carried[None],
        stacked[0],
        stacked[1],
        stacked[2],
        stacked[3],
        stacked[4],
        stacked[5],
        stacked[6],
        stacked[7],
        stacked[8],
    )


def solution(mesh):
    placed = (
        P(("rep", "fsdp"), "ctx", None),
        P(("rep", "fsdp")),
        P(("rep", "fsdp"), "ctx", None),
        P(None, None, "fsdp", None),
        P(None, "fsdp", None),
        P(None, "fsdp", None),
        P(None, "fsdp", None),
        P(None, "fsdp"),
        P(None, None, "fsdp"),
        P(None, "fsdp"),
        P(None, None, "fsdp"),
        P(None, None, "fsdp"),
    )
    return jax.shard_map(
        body,
        mesh=mesh,
        in_specs=placed,
        out_specs=(
            P(("rep", "fsdp"), "ctx", None),
            P(("rep", "fsdp"), "ctx", None),
            P(None, None, "fsdp", None),
            P(None, "fsdp", None),
            P(None, "fsdp", None),
            P(None, "fsdp", None),
            P(None, "fsdp"),
            P(None, None, "fsdp"),
            P(None, "fsdp"),
            P(None, None, "fsdp"),
            P(None, None, "fsdp"),
        ),
        check_vma=False,
    )
```

profile of v0, /device:TPU:0, one launch (start us, length us, event | category | flops | bytes accessed | tf_op | source)
XLA Modules:
  0.0 1759.2 jit_solution(700150922769034059)
XLA Ops:
  10.9 17.6 %all-gather.1 = bf16[1,3,768]{1,0,2:T(2,128)(2,1)S(1)} all-gather(bf16[1,3,192]{1,0,2:T(2,128)(2,1)S(1)} %copy.126), channel_id=3, replica_groups=mesh['rep'=2,'fsdp'=4,'ctx'=4] {'fsdp'}, dimensions={2}, use_global_device_ids=true | all-gather | bytes 5760 | tf_op jit(solution)/shard_map/all_gather | solution.py:268
  36.3 47.7 %all-gather.39.cloned.1.call-done = bf16[1,3,768,768]{3,2,1,0:T(8,128)(2,1)} async-done(((bf16[1,3,192,768]{3,2,1,0:T(8,128)(2,1)}), bf16[1,3,768,768]{3,2,1,0:T(8,128)(2,1)}) %all-gather.39.cloned.1.call-update) | async-done | bytes 3538960 | tf_op jit(solution)/shard_map/all_gather | solution.py:263
  130.5 16.3 all-gather.5
  173.0 28.9 %while.56 = (s32[]{:T(128)}, bf16[6,256,128]{1,2,0:T(8,128)(2,1)S(1)}, f32[6,2,256]{2,1,0:T(2,128)S(1)}, s32[6]{0:T(128)S(1)}, bf16[1024,768]{0,1:T(8,128)(2,1)S...) while((s32[]{:T(128)}, ...), condition=%wide.region_3.4_spmd.clone, body=%wide.region_0.3_spmd.clone.sunk | while | flops 140509696 | bytes 8278211 | solution.py:67
  204.7 47.2 %all-gather.43.cloned.1.call-done = bf16[1,768,3072]{2,1,0:T(8,128)(2,1)} async-done(((bf16[1,192,3072]{2,1,0:T(8,128)(2,1)}), bf16[1,768,3072]{2,1,0:T(8,128)(2,1)}) %all-gather.43.cloned.1.call-update) | async-done | bytes 4718608 | tf_op jit(solution)/shard_map/all_gather | solution.py:265
  263.6 77.7 %all-gather.45.cloned.1.call-done = bf16[1,3072,768]{2,1,0:T(8,128)(2,1)} async-done(((bf16[1,768,768]{2,1,0:T(8,128)(2,1)}), bf16[1,3072,768]{2,1,0:T(8,128)(2,1)}) %all-gather.45.cloned.1.call-update) | async-done | bytes 4718608 | tf_op jit(solution)/shard_map/all_gather | solution.py:266
  346.6 64.6 %all-gather.47.cloned.1.call-done = bf16[1,3,768,768]{3,2,1,0:T(8,128)(2,1)} async-done(((bf16[1,3,192,768]{3,2,1,0:T(8,128)(2,1)}), bf16[1,3,768,768]{3,2,1,0:T(8,128)(2,1)}) %all-gather.47.cloned.1.call-update) | async-done | bytes 3538960 | tf_op jit(solution)/shard_map/all_gather | solution.py:263
  414.0 15.2 all-gather.10
  461.9 16.9 all-gather.14
  504.3 29.4 %while.57 = (s32[]{:T(128)}, bf16[6,256,128]{1,2,0:T(8,128)(2,1)S(1)}, f32[6,2,256]{2,1,0:T(2,128)S(1)}, s32[6]{0:T(128)S(1)}, bf16[1024,768]{0,1:T(8,128)(2,1)}...) while((s32[]{:T(128)}, ...), condition=%wide.region_11.12_spmd.clone, body=%wide.region_8.11_spmd.clone.sunk | while | flops 140509696 | bytes 8278211 | solution.py:67
  537.2 45.4 %all-gather.51.cloned.1.call-done = bf16[1,768,3072]{2,1,0:T(8,128)(2,1)} async-done(((bf16[1,192,3072]{2,1,0:T(8,128)(2,1)}), bf16[1,768,3072]{2,1,0:T(8,128)(2,1)}) %all-gather.51.cloned.1.call-update) | async-done | bytes 4718608 | tf_op jit(solution)/shard_map/all_gather | solution.py:265
  594.6 77.3 %all-gather.53.cloned.1.call-done = bf16[1,3072,768]{2,1,0:T(8,128)(2,1)} async-done(((bf16[1,768,768]{2,1,0:T(8,128)(2,1)}), bf16[1,3072,768]{2,1,0:T(8,128)(2,1)}) %all-gather.53.cloned.1.call-update) | async-done | bytes 4718608 | tf_op jit(solution)/shard_map/all_gather | solution.py:266
  688.4 58.5 %while.58 = (s32[]{:T(128)}, bf16[6,256,128]{1,2,0:T(8,128)(2,1)}, bf16[6,1024,128]{1,2,0:T(8,128)(2,1)}, bf16[6,1024,128]{1,2,0:T(8,128)(2,1)}, s32[6]{0:T(128)...) while((s32[]{:T(128)}, bf16[6,256,128]{1,2,0:T(8,128)(2,1)}, ...), condition=%wide.region_22.23_spmd.clone, body=%wide.region_20.22_spmd.clone.sunk | while | flops 340591104 | bytes 20002016 | solution.py:108
  750.7 23.0 %reduce-scatter.35.cloned.1.call-done = bf16[256,768]{0,1:T(8,128)(2,1)} async-done(((bf16[1024,768]{0,1:T(8,128)(2,1)}), bf16[256,768]{0,1:T(8,128)(2,1)}) %reduce-scatter.35.cloned.1.call-update) | async-done | bytes 393232 | tf_op jit(solution)/shard_map/reduce_scatter | solution.py:200
  776.7 27.8 %reduce-scatter.37.cloned.1.call-done = bf16[256,768]{0,1:T(8,128)(2,1)} async-done(((bf16[1024,768]{0,1:T(8,128)(2,1)}), bf16[256,768]{0,1:T(8,128)(2,1)}) %reduce-scatter.37.cloned.1.call-update) | async-done | bytes 393232 | tf_op jit(solution)/shard_map/reduce_scatter | solution.py:203
  822.0 56.9 %while.59 = (s32[]{:T(128)}, bf16[6,256,128]{1,2,0:T(8,128)(2,1)}, bf16[6,1024,128]{1,2,0:T(8,128)(2,1)}, bf16[6,1024,128]{1,2,0:T(8,128)(2,1)}, s32[6]{0:T(128)...) while((s32[]{:T(128)}, bf16[6,256,128]{1,2,0:T(8,128)(2,1)}, ...), condition=%wide.region_31.32_spmd.clone, body=%wide.region_29.31_spmd.clone.sunk | while | flops 340591104 | bytes 20002016 | solution.py:108
  909.8 28.8 %reduce-scatter.41.cloned.1.call-done = bf16[256,768]{0,1:T(8,128)(2,1)} async-done(((bf16[1024,768]{0,1:T(8,128)(2,1)}), bf16[256,768]{0,1:T(8,128)(2,1)}) %reduce-scatter.41.cloned.1.call-update) | async-done | bytes 393232 | tf_op jit(solution)/shard_map/reduce_scatter | solution.py:203
  987.3 20.4 %reduce-scatter.57.cloned.1.call-done = bf16[192,2304]{1,0:T(8,128)(2,1)} async-done(((bf16[768,2304]{1,0:T(8,128)(2,1)}), bf16[192,2304]{1,0:T(8,128)(2,1)}) %reduce-scatter.57.cloned.1.call-update) | async-done | bytes 884752
  1012.0 64.6 %reduce-scatter.55.cloned.1.call-done = bf16[192,2304]{1,0:T(8,128)(2,1)} async-done(((bf16[768,2304]{1,0:T(8,128)(2,1)}), bf16[192,2304]{1,0:T(8,128)(2,1)}) %reduce-scatter.55.cloned.1.call-update) | async-done | bytes 884752
  1080.9 27.5 %reduce-scatter.45.cloned.1.call-done = bf16[192,768]{1,0:T(8,128)(2,1)} async-done(((bf16[768,768]{1,0:T(8,128)(2,1)}), bf16[192,768]{1,0:T(8,128)(2,1)}) %reduce-scatter.45.cloned.1.call-update) | async-done | bytes 294928 | tf_op jit(solution)/shard_map/reduce_scatter | solution.py:298
  1108.4 30.1 %reduce-scatter.43.cloned.1.call-done = bf16[192,768]{1,0:T(8,128)(2,1)} async-done(((bf16[768,768]{1,0:T(8,128)(2,1)}), bf16[192,768]{1,0:T(8,128)(2,1)}) %reduce-scatter.43.cloned.1.call-update) | async-done | bytes 294928 | tf_op jit(solution)/shard_map/reduce_scatter | solution.py:298
  1138.5 86.9 %reduce-scatter.49.cloned.1.call-done = bf16[192,3072]{1,0:T(8,128)(2,1)} async-done(((bf16[768,3072]{1,0:T(8,128)(2,1)}), bf16[192,3072]{1,0:T(8,128)(2,1)}) %reduce-scatter.49.cloned.1.call-update) | async-done | bytes 1179664 | tf_op jit(solution)/shard_map/reduce_scatter | solution.py:301
  1225.4 88.1 %reduce-scatter.53.cloned.1.call-done = bf16[768,768]{1,0:T(8,128)(2,1)} async-done(((bf16[3072,768]{1,0:T(8,128)(2,1)}), bf16[768,768]{1,0:T(8,128)(2,1)}) %reduce-scatter.53.cloned.1.call-update) | async-done | bytes 1179664 | tf_op jit(solution)/shard_map/reduce_scatter | solution.py:304
  1313.5 88.7 %reduce-scatter.47.cloned.1.call-done = bf16[192,3072]{1,0:T(8,128)(2,1)} async-done(((bf16[768,3072]{1,0:T(8,128)(2,1)}), bf16[192,3072]{1,0:T(8,128)(2,1)}) %reduce-scatter.47.cloned.1.call-update) | async-done | bytes 1179664 | tf_op jit(solution)/shard_map/reduce_scatter | solution.py:301
  1402.2 88.0 %reduce-scatter.51.cloned.1.call-done = bf16[768,768]{1,0:T(8,128)(2,1)} async-done(((bf16[3072,768]{1,0:T(8,128)(2,1)}), bf16[768,768]{1,0:T(8,128)(2,1)}) %reduce-scatter.51.cloned.1.call-update) | async-done | bytes 1179664 | tf_op jit(solution)/shard_map/reduce_scatter | solution.py:304
  1492.5 19.8 %reduce-scatter.65.cloned.1.call-done = bf16[192,2]{1,0:T(8,128)(2,1)} async-done(((bf16[768,2]{1,0:T(8,128)(2,1)}), bf16[192,2]{1,0:T(8,128)(2,1)}) %reduce-scatter.65.cloned.1.call-update) | async-done | bytes 784
  1513.2 18.9 %reduce-scatter.69.cloned.1.call-done = bf16[192,2]{1,0:T(8,128)(2,1)} async-done(((bf16[768,2]{1,0:T(8,128)(2,1)}), bf16[192,2]{1,0:T(8,128)(2,1)}) %reduce-scatter.69.cloned.1.call-update) | async-done | bytes 784
  1534.2 15.8 all-reduce.8
  1553.2 18.6 %reduce-scatter.67.cloned.1.call-done = bf16[192,2]{1,0:T(8,128)(2,1)} async-done(((bf16[768,2]{1,0:T(8,128)(2,1)}), bf16[192,2]{1,0:T(8,128)(2,1)}) %reduce-scatter.67.cloned.1.call-update) | async-done | bytes 784
  1572.7 19.0 %reduce-scatter.61.cloned.1.call-done = bf16[192,3]{1,0:T(8,128)(2,1)} async-done(((bf16[768,3]{1,0:T(8,128)(2,1)}), bf16[192,3]{1,0:T(8,128)(2,1)}) %reduce-scatter.61.cloned.1.call-update) | async-done | bytes 1168
  1612.4 23.3 %all-reduce.6 = (bf16[1,192]{1,0:T(2,128)(2,1)S(1)}, bf16[1,192]{1,0:T(2,128)(2,1)S(1)}, bf16[1,3,192]{2,1,0:T(4,128)(2,1)S(1)}, bf16[1,3,192]{2,1,0:T(4,128)(2,...) all-reduce(bf16[1,192]{1,0:T(2,128)(2,1)S(1)} %stack.247, ...), channel_id=1, replica_groups=mesh['rep'=2,'fsdp'=4,'ctx'=4] {'rep','ctx'}, use_global_device_ids=true, to_apply=%region_55.56 | all-reduce | flops 4608 | bytes 18432 | tf_op jit(solution)/shard_map/psum | solution.py:328
  1638.1 97.4 %all-reduce.12.cloned.1.call-done = (bf16[1,3,192,768]{2,3,1,0:T(8,128)(2,1)}, bf16[1,3,192,768]{2,3,1,0:T(8,128)(2,1)}, bf16[1,192,768]{2,1,0:T(8,128)(2,1)}, b...) async-done(((bf16[1,3,192,768]{2,3,1,0:T(8,128)(2,1)}, ...) | async-done | bytes 7077904 | tf_op jit(solution)/shard_map/psum | solution.py:324
  (702 shorter events, 510.7 us)
Async XLA Ops:
  7.2 76.9 %all-gather.39.cloned.1.call-start = ((), (), s32[]{:S(2)}) async-start(), calls=%async_computation.32 | async-start | bytes 4423680 | tf_op jit(solution)/shard_map/all_gather | solution.py:263
  10.1 158.4 %all-gather.31.cloned.1.call-start = ((), (), s32[]{:S(2)}) async-start(), calls=%async_computation.18 | async-start | bytes 1966080 | tf_op jit(solution)/shard_map/all_gather | solution.py:129
  86.6 83.7 %all-gather.33.cloned.1.call-start = ((), (), s32[]{:S(2)}) async-start(), calls=%async_computation.19 | async-start | bytes 1966080 | tf_op jit(solution)/shard_map/all_gather | solution.py:128
  89.2 112.9 %all-gather.41.cloned.1.call-start = ((), (), s32[]{:S(2)}) async-start(), calls=%async_computation.33 | async-start | bytes 1474560 | tf_op jit(solution)/shard_map/all_gather | solution.py:264
  90.1 161.8 %all-gather.43.cloned.1.call-start = ((), (), s32[]{:S(2)}) async-start(), calls=%async_computation.34 | async-start | bytes 5898240 | tf_op jit(solution)/shard_map/all_gather | solution.py:265
  93.5 247.8 %all-gather.45.cloned.1.call-start = ((), (), s32[]{:S(2)}) async-start(), calls=%async_computation.35 | async-start | bytes 5898240 | tf_op jit(solution)/shard_map/all_gather | solution.py:266
  96.7 314.5 %all-gather.47.cloned.1.call-start = ((), (), s32[]{:S(2)}) async-start(), calls=%async_computation.36 | async-start | bytes 4423680 | tf_op jit(solution)/shard_map/all_gather | solution.py:263
  97.5 401.5 %all-gather.37.cloned.1.call-start = ((), (), s32[]{:S(2)}) async-start(), calls=%async_computation.21 | async-start | bytes 1966080 | tf_op jit(solution)/shard_map/all_gather | solution.py:128
  151.7 189.5 %copy-start.41 = (f32[768]{0:T(1024)}, f32[768]{0:T(1024)S(1)}, u32[]{:S(2)}) copy-start(f32[768]{0:T(1024)S(1)} %get-tuple-element.531) | copy-start | bytes 9220
  413.7 87.9 %all-gather.35.cloned.1.call-start = ((), (), s32[]{:S(2)}) async-start(), calls=%async_computation.20 | async-start | bytes 1966080 | tf_op jit(solution)/shard_map/all_gather | solution.py:129
  439.6 94.2 %all-gather.49.cloned.1.call-start = ((), (), s32[]{:S(2)}) async-start(), calls=%async_computation.37 | async-start | bytes 1474560 | tf_op jit(solution)/shard_map/all_gather | solution.py:264
  440.2 142.4 %all-gather.51.cloned.1.call-start = ((), (), s32[]{:S(2)}) async-start(), calls=%async_computation.38 | async-start | bytes 5898240 | tf_op jit(solution)/shard_map/all_gather | solution.py:265
  440.9 231.0 %all-gather.53.cloned.1.call-start = ((), (), s32[]{:S(2)}) async-start(), calls=%async_computation.39 | async-start | bytes 5898240 | tf_op jit(solution)/shard_map/all_gather | solution.py:266
  441.5 332.2 %reduce-scatter.35.cloned.1.call-start = ((), (), s32[]{:S(2)}) async-start(), calls=%async_computation.22 | async-start | bytes 1966080 | tf_op jit(solution)/shard_map/reduce_scatter | solution.py:200
  746.9 57.6 %reduce-scatter.37.cloned.1.call-start = ((), (), s32[]{:S(2)}) async-start(), calls=%async_computation.23 | async-start | bytes 1966080 | tf_op jit(solution)/shard_map/reduce_scatter | solution.py:203
  747.5 159.8 %reduce-scatter.39.cloned.1.call-start = ((), (), s32[]{:S(2)}) async-start(), calls=%async_computation.24 | async-start | bytes 1966080 | tf_op jit(solution)/shard_map/reduce_scatter | solution.py:200
  878.9 59.7 %reduce-scatter.41.cloned.1.call-start = ((), (), s32[]{:S(2)}) async-start(), calls=%async_computation.25 | async-start | bytes 1966080 | tf_op jit(solution)/shard_map/reduce_scatter | solution.py:203
  879.5 128.2 %reduce-scatter.57.cloned.1.call-start = ((), (), s32[]{:S(2)}) async-start(), calls=%async_computation.41 | async-start | bytes 4423680
  890.5 186.1 %reduce-scatter.55.cloned.1.call-start = ((), (), s32[]{:S(2)}) async-start(), calls=%async_computation.40 | async-start | bytes 4423680
  956.2 152.2 %reduce-scatter.45.cloned.1.call-start = ((), (), s32[]{:S(2)}) async-start(), calls=%async_computation.27 | async-start | bytes 1474560 | tf_op jit(solution)/shard_map/reduce_scatter | solution.py:298
  958.9 179.6 %reduce-scatter.43.cloned.1.call-start = ((), (), s32[]{:S(2)}) async-start(), calls=%async_computation.26 | async-start | bytes 1474560 | tf_op jit(solution)/shard_map/reduce_scatter | solution.py:298
  960.5 264.9 %reduce-scatter.49.cloned.1.call-start = ((), (), s32[]{:S(2)}) async-start(), calls=%async_computation.29 | async-start | bytes 5898240 | tf_op jit(solution)/shard_map/reduce_scatter | solution.py:301
  965.7 347.7 %reduce-scatter.53.cloned.1.call-start = ((), (), s32[]{:S(2)}) async-start(), calls=%async_computation.31 | async-start | bytes 5898240 | tf_op jit(solution)/shard_map/reduce_scatter | solution.py:304
  970.8 431.4 %reduce-scatter.47.cloned.1.call-start = ((), (), s32[]{:S(2)}) async-start(), calls=%async_computation.28 | async-start | bytes 5898240 | tf_op jit(solution)/shard_map/reduce_scatter | solution.py:301
  975.9 514.2 %reduce-scatter.51.cloned.1.call-start = ((), (), s32[]{:S(2)}) async-start(), calls=%async_computation.30 | async-start | bytes 5898240 | tf_op jit(solution)/shard_map/reduce_scatter | solution.py:304
  981.1 531.2 %reduce-scatter.65.cloned.1.call-start = ((), (), s32[]{:S(2)}) async-start(), calls=%async_computation.45 | async-start | bytes 245760
  982.1 550.1 %reduce-scatter.69.cloned.1.call-start = ((), (), s32[]{:S(2)}) async-start(), calls=%async_computation.47 | async-start | bytes 245760
  983.0 569.3 %reduce-scatter.63.cloned.1.call-start = ((), (), s32[]{:S(2)}) async-start(), calls=%async_computation.44 | async-start | bytes 245760
  984.0 587.8 %reduce-scatter.67.cloned.1.call-start = ((), (), s32[]{:S(2)}) async-start(), calls=%async_computation.46 | async-start | bytes 245760
  985.2 606.5 %reduce-scatter.61.cloned.1.call-start = ((), (), s32[]{:S(2)}) async-start(), calls=%async_computation.43 | async-start | bytes 245760
  986.1 625.4 %reduce-scatter.59.cloned.1.call-start = ((), (), s32[]{:S(2)}) async-start(), calls=%async_computation.42 | async-start | bytes 245760
  987.3 748.3 %all-reduce.12.cloned.1.call-start = ((), (), s32[]{:S(2)}) async-start(), calls=%async_computation.48 | async-start | bytes 15335424 | tf_op jit(solution)/shard_map/psum | solution.py:324
  (68 other events, 1276.0 us)
Sparse Core Ops, SparseCore 0:
  10.2 73.8 all-gather.38
  86.7 18.4 all-gather.30
  107.4 19.6 all-gather.32
  129.1 31.4 all-gather.40
  162.6 89.2 all-gather.42
  253.3 87.8 all-gather.44
  342.8 68.3 all-gather.46
  413.9 18.2 all-gather.36
  439.7 17.9 all-gather.34
  459.1 32.1 all-gather.48
  493.5 89.0 all-gather.50
  584.0 87.8 all-gather.52
  747.0 26.6 reduce-scatter.34
  776.2 28.1 reduce-scatter.36
  879.1 28.1 reduce-scatter.38
  910.4 28.1 reduce-scatter.40
  941.3 66.3 reduce-scatter.56
  1009.9 66.6 reduce-scatter.54
  1078.9 29.4 reduce-scatter.44
  1110.6 27.8 reduce-scatter.42
  1141.4 83.9 reduce-scatter.48
  1227.7 85.7 reduce-scatter.52
  1316.4 85.7 reduce-scatter.46
  1404.3 85.7 reduce-scatter.50
  1492.4 19.8 reduce-scatter.64
  1514.5 17.5 reduce-scatter.68
  1534.2 17.5 reduce-scatter.62
  1554.2 17.6 reduce-scatter.66
  1574.1 17.5 reduce-scatter.60
  1593.9 17.5 reduce-scatter.58
  1616.3 119.2 all-reduce.11
where the time goes:
time: 1770 us; the launch traced here: 1760 us
  waiting for transfers between devices  1140 us (64%)
  local copies, waits for them, and re-layouts  191 us (11%)
  blocking collectives  171 us (10%)
  matrix products  152 us (9%)
  other arithmetic  66.8 us (4%)
  between operations  18.7 us (1%)
    unnamed x39, waiting for transfers between devices  180 us
    reduce_scatter x2, waiting for transfers between devices, body(): lax.psum_scatter(grads_block[3].astype(jnp.bfloat16), 'fsdp', scatter_dim...  176 us
    reduce_scatter x2, waiting for transfers between devices, body(): lax.psum_scatter(grads_block[2].astype(jnp.bfloat16), 'fsdp', scatter_dim...  176 us
    all_gather x2, waiting for transfers between devices, body(): lax.all_gather(w_out[layer_idx], 'fsdp', axis=0, tiled=True)  155 us
    all_gather x2, waiting for transfers between devices, body(): lax.all_gather(w_qkv[layer_idx], 'fsdp', axis=1, tiled=True)  112 us
    psum x1, waiting for transfers between devices, body(): lax.psum(shard_sums[0].astype(jnp.bfloat16), ('rep', 'ctx'))  97.4 us
    all_gather x2, waiting for transfers between devices, body(): lax.all_gather(w_in[layer_idx], 'fsdp', axis=0, tiled=True)  92.6 us
    unnamed x181, local copies, waits for them, and re-layouts  66 us
  transfers between devices with their start and end apart: 31, of which 24 were waited for; matrix products, arithmetic and copies ran while one was open for 14% of the time, Pallas kernels for 0%

commit v1 on v0

--- a/solution.py
+++ b/solution.py
@@ -1,15 +1,588 @@
+import functools
+
 import jax
 import jax.numpy as jnp
 from jax import lax
+from jax.experimental import pallas as pl
+from jax.experimental.pallas import tpu as pltpu
 from jax.sharding import PartitionSpec as P
 
 HEADS = 12
 HEAD = 64
-
+D = HEADS * HEAD
+MESH = pl.DeviceIdType.MESH
+BF = jnp.bfloat16
+F32 = jnp.float32
+MIB = 2**20
 
 epsilon = 1e-05
 score_scale = 0.125
 masked_value = -1e30
+
+
+class Place:
+    def __init__(self, n, ny):
+        self.n, self.ny = n, ny
+        self.r = lax.axis_index("rep")
+        self.z = lax.axis_index("fsdp")
+        c = lax.axis_index("ctx")
+        self.y, self.k = lax.div(c, 2), lax.rem(c, 2)
+        self.p = lax.rem(self.r + self.y, 2)
+
+    def shard(self, offset):
+        return lax.rem(self.z + (offset + self.n), self.n)
+
+    def at(self, dr=0, dz=0, dy=0, dk=0):
+        r = lax.rem(self.r + dr, 2)
+        y = lax.rem(self.y + (dy + self.ny), self.ny)
+        k = lax.rem(self.k + dk, 2)
+        return (r, self.shard(dz), 2 * y + k)
+
+    def greet(self, others):
+        barrier = pltpu.get_barrier_semaphore()
+        for other in others:
+            pl.semaphore_signal(barrier, inc=1, device_id=other, device_id_type=MESH)
+        pl.semaphore_wait(barrier, len(others))
+
+    def everyone(self):
+        others = [self.at(dz=o) for o in range(1, self.n)]
+        others += [self.at(dr=1), self.at(dk=1)]
+        others += [self.at(dy=o) for o in range(1, self.ny)]
+        return others
+
+
+def remote(src, dst, send, recv, device):
+    copy = pltpu.make_async_remote_copy(
+        src_ref=src, dst_ref=dst, send_sem=send, recv_sem=recv, device_id=device, device_id_type=MESH
+    )
+    copy.start()
+    return copy
+
+
+class Gather:
+    def __init__(self, place, full, by_shard, local, send, recv):
+        self.place, self.full, self.by_shard = place, full, by_shard
+        self.local, self.send, self.recv = local, send, recv
+        self.n = place.n
+        self.half = full.shape[2] // 2
+        self.copies = []
+        self.core_copies = []
+
+    @staticmethod
+    def count(n):
+        return 6 * n - 4
+
+    def part(self, shard, q0, count, k):
+        rows = pl.ds(pl.multiple_of(k * self.half, self.half), self.half)
+        if self.by_shard:
+            return self.full.at[shard, pl.ds(q0, count), rows]
+        return self.full.at[pl.ds(q0, count), shard, rows]
+
+    def load(self, sources):
+        self.loads = []
+        for i, (q, count, source) in enumerate(sources):
+            z = self.place.z
+            if self.by_shard:
+                target = self.full.at[z]
+            elif count is None:
+                target = self.full.at[q, z]
+            else:
+                target = self.full.at[pl.ds(q, count), z]
+            copy = pltpu.make_async_copy(source, target, self.local.at[i])
+            copy.start()
+            self.loads.append(copy)
+
+    def share(self, piece, slot, device, core=False):
+        copy = remote(piece, piece, self.send.at[slot], self.recv.at[slot], device)
+        (self.core_copies if core else self.copies).append(copy)
+        return copy
+
+    def core_share(self, shard, q0, count, slot):
+        place = self.place
+        base = self.n + 2 * (self.n - 1)
+        self.share(self.part(shard, q0, count, place.k), base + slot, place.at(dk=1), core=True)
+
+    def start(self):
+        place, n = self.place, self.n
+        for copy in self.loads:
+            copy.wait()
+        self.plus, self.minus = {}, {}
+        self.xs, self.ys = {}, {}
+        mine = self.part(place.z, 2 * place.p, 2, place.k)
+        if n // 2 > 1:
+            self.plus[1] = self.share(mine, 0, place.at(dz=1))
+            self.minus[1] = self.share(mine, n // 2, place.at(dz=-1))
+        else:
+            self.plus[1] = self.share(self.part(place.z, 2 * place.p, 1, place.k), 0, place.at(dz=1))
+            self.minus[1] = self.share(self.part(place.z, 2 * place.p + 1, 1, place.k), 1, place.at(dz=-1))
+
+    def hop(self, d, forward):
+        place, n = self.place, self.n
+        sign = 1 if forward else -1
+        table = self.plus if forward else self.minus
+        table[d].wait_recv()
+        shard = place.shard(-sign * d)
+        q0 = 2 * place.p + (0 if forward else 1)
+        base = 0 if forward else n // 2
+        if d < n // 2:
+            if d + 1 < n // 2:
+                piece = self.part(shard, 2 * place.p, 2, place.k)
+            else:
+                piece = self.part(shard, q0, 1, place.k)
+            table[d + 1] = self.share(piece, base + d, place.at(dz=sign))
+        whole = d < n // 2
+        distance = (sign * d) % n
+        if whole or forward:
+            slot = n + distance - 1
+            self.xs[distance] = self.share(self.part(shard, 2 * place.p, 1, place.k), slot, place.at(dr=1))
+        if whole or not forward:
+            slot = n + (n - 1) + distance - 1
+            self.ys[distance] = self.share(self.part(shard, 2 * place.p + 1, 1, place.k), slot, place.at(dy=1))
+        if whole:
+            self.core_share(shard, 2 * place.p, 2, base + d - 1)
+        else:
+            self.core_share(shard, q0, 1, base + d - 1)
+
+    def hops(self, d):
+        self.hop(d, True)
+        self.hop(d, False)
+
+    def cross(self, which):
+        place, n = self.place, self.n
+        table = (self.xs, self.ys)[which]
+        for distance in sorted(table, key=lambda o: min(o, n - o)):
+            table[distance].wait_recv()
+            shard = place.shard(-distance)
+            q = 2 * (1 - place.p) + which
+            self.core_share(shard, q, 1, n + which * (n - 1) + distance - 1)
+
+    def finish(self):
+        for copy in self.core_copies:
+            copy.wait_recv()
+
+    def drain(self):
+        for copy in self.core_copies + self.copies:
+            copy.wait_send()
+
+    def steps(self):
+        out = [self.start]
+        out += [functools.partial(self.hops, d) for d in range(1, self.n // 2 + 1)]
+        out += [functools.partial(self.cross, 0), functools.partial(self.cross, 1), self.finish]
+        return out
+
+
+def weight_sources(b, qkv, ao, win, wout):
+    return [
+        [(0, 3, qkv.at[b]), (3, None, ao.at[b])],
+        [(q, None, win.at[b, :, pl.ds(q * D, D)]) for q in range(4)],
+        [(None, None, wout.at[b])],
+    ]
+
+
+def gather_kernel(n, ny, *refs):
+    qkv, ao, win, wout, small = refs[:5]
+    fulls, small_full = refs[5:11], refs[11]
+    local, send, recv, small_send, small_recv = refs[12:]
+    place = Place(n, ny)
+    groups = []
+    for g in range(6):
+        b, kind = g // 3, g % 3
+        group = Gather(place, fulls[g], kind == 2, local.at[g], send.at[g], recv.at[g])
+        group.load(weight_sources(b, qkv, ao, win, wout)[kind])
+        groups.append(group)
+    own = pltpu.make_async_copy(small, small_full.at[place.z], small_send.at[0])
+    own.start()
+    place.greet(place.everyone())
+    smalls = [
+        remote(small, small_full.at[place.z], small_send.at[o], small_recv.at[o], place.at(dz=o))
+        for o in range(1, n)
+    ]
+    steps = [group.steps() for group in groups]
+    for t in range(len(steps[0]) + 5):
+        for g in range(6):
+            if 0 <= t - g < len(steps[g]):
+                steps[g][t - g]()
+    for group in groups:
+        group.drain()
+    own.wait()
+    for copy in smalls:
+        copy.wait()
+
+
+def gather_weights(n, ny, qkv, ao, win, wout, small):
+    rows = D // n
+    shapes = [(4, n, rows, D), (4, n, rows, D), (n, 4, rows, D)] * 2
+    out = [jax.ShapeDtypeStruct(shape, BF) for shape in shapes]
+    out.append(jax.ShapeDtypeStruct((n,) + small.shape, BF))
+    anywhere = pl.BlockSpec(memory_space=pl.ANY)
+    return pl.pallas_call(
+        functools.partial(gather_kernel, n, ny),
+        out_shape=out,
+        in_specs=[anywhere] * 5,
+        out_specs=[anywhere] * 7,
+        scratch_shapes=[
+            pltpu.SemaphoreType.DMA((6, 4)),
+            pltpu.SemaphoreType.DMA((6, Gather.count(n))),
+            pltpu.SemaphoreType.DMA((6, Gather.count(n))),
+            pltpu.SemaphoreType.DMA((n,)),
+            pltpu.SemaphoreType.DMA((n,)),
+        ],
+        compiler_params=pltpu.CompilerParams(collective_id=0, has_side_effects=True),
+        name="gather_weights",
+    )(qkv, ao, win, wout, small)
+
+
+class Reduce:
+    def __init__(self, place, by_shard, slot, landing, local, send, recv):
+        self.place, self.by_shard = place, by_shard
+        self.half_in, self.plane_out, self.total = slot
+        self.core_in, self.ring_in, self.plane_in = landing
+        self.local, self.send, self.recv = local, send, recv
+        self.n, self.ny = place.n, place.ny
+        self.half = self.half_in.shape[2]
+        self.copies, self.owns = [], []
+        self.rings, self.planes = {}, {}
+
+    @staticmethod
+    def count(n, ny):
+        return 4 + n + 2 * ny + 4
+
+    @staticmethod
+    def slot_buffers(n):
+        half = D // n // 2
+        return [pltpu.VMEM((n, 4, half, D), BF), pltpu.VMEM((2, 4, half, D), BF), pltpu.VMEM((4, half, D), F32)]
+
+    @staticmethod
+    def landing_buffers(n, ny):
+        half = D // n // 2
+        return [
+            pltpu.VMEM((n, 4, half, D), BF),
+            pltpu.VMEM((2, n // 2, 4, half, D), BF),
+            pltpu.VMEM((2 * ny, 2, half, D), BF),
+        ]
+
+    def parts_of(self, grad, k):
+        rows = pl.ds(pl.multiple_of(k * self.half, self.half), self.half)
+        if self.by_shard:
+            return [(pl.ds(0, 4), grad.at[:, :, rows])]
+        return [(q, grad.at[q, :, rows]) for q in range(4)]
+
+    def load(self, grad):
+        self.loaded = []
+        for i, (q, part) in enumerate(self.parts_of(grad, self.place.k)):
+            copy = pltpu.make_async_copy(part, self.half_in.at[:, q], self.local.at[4 + i])
+            copy.start()
+            self.loaded.append(copy)
+
+    def core(self, grad):
+        self.cored = []
+        for i, (q, part) in enumerate(self.parts_of(grad, 1 - self.place.k)):
+            copy = remote(
+                part, self.core_in.at[:, q], self.send.at[i], self.recv.at[i], self.place.at(dk=1)
+            )
+            self.cored.append(copy)
+            self.copies.append(copy)
+
+    def ring_send(self, d):
+        place, n = self.place, self.n
+        for sign in (1, -1):
+            way = 0 if sign == 1 else 1
+            shard = place.shard(sign * d)
+            if d == n // 2:
+                q0, count = 2 * way, 2
+            else:
+                q0, count = 0, 4
+            slot = 4 + way * (n // 2) + d - 1
+            copy = remote(
+                self.half_in.at[shard, pl.ds(q0, count)],
+                self.ring_in.at[way, d - 1, pl.ds(q0, count)],
+                self.send.at[slot],
+                self.recv.at[slot],
+                place.at(dz=sign),
+            )
+            self.rings[(way, d)] = copy
+            self.copies.append(copy)
+
+    def add_into(self, target, source):
+        target[...] = (target[...].astype(F32) + source[...].astype(F32)).astype(BF)
+
+    def add_cores(self):
+        for copy in self.loaded:
+            copy.wait()
+        for copy in self.cored:
+            copy.wait_recv()
+
+        def one(i, _):
+            shard, q = lax.div(i, 4), lax.rem(i, 4)
+            self.add_into(self.half_in.at[shard, q], self.core_in.at[shard, q])
+            return 0
+
+        lax.fori_loop(0, 4 * self.n, one, 0)
+        self.ring_send(self.n // 2)
+
+    def ring_step(self, d):
+        place, n = self.place, self.n
+        for sign in (1, -1):
+            way = 0 if sign == 1 else 1
+            self.rings[(way, d + 1)].wait_recv()
+            shard = place.shard(sign * d)
+            qs = range(4) if d + 1 < n // 2 else range(2 * way, 2 * way + 2)
+            for q in qs:
+                self.add_into(self.half_in.at[shard, q], self.ring_in.at[way, d, q])
+        self.ring_send(d)
+
+    def ring_end(self):
+        place = self.place
+        for way in (0, 1):
+            self.rings[(way, 1)].wait_recv()
+        for q in range(4):
+            total = self.half_in[place.z, q].astype(F32)
+            for way in (0, 1):
+                if self.n > 2 or q // 2 == way:
+                    total = total + self.ring_in[way, 0, q].astype(F32)
+            self.plane_out[0, q] = total.astype(BF)
+        self.plane_send(0)
+
+    def plane_send(self, turn):
+        place, ny = self.place, self.ny
+        base = 4 + self.n + turn * ny
+        slot = base
+        qx = 2 * turn
+        copy = remote(
+            self.plane_out.at[turn, pl.ds(qx, 2)],
+            self.plane_in.at[turn * ny],
+            self.send.at[slot],
+            self.recv.at[slot],
+            place.at(dr=1),
+        )
+        self.planes[(turn, 0)] = copy
+        self.copies.append(copy)
+        for o in range(1, ny):
+            copy = remote(
+                self.plane_out.at[turn, pl.ds(2 - qx, 2)],
+                self.plane_in.at[turn * ny + o],
+                self.send.at[slot + o],
+                self.recv.at[slot + o],
+                place.at(dy=o),
+            )
+            self.planes[(turn, o)] = copy
+            self.copies.append(copy)
+
+    def plane_sum(self, turn, q):
+        place, ny = self.place, self.ny
+        over_x = (q // 2 == 0) == (turn == 0)
+        own = self.plane_out[turn, q].astype(F32)
+        if over_x:
+            return own + self.plane_in[turn * ny, q % 2].astype(F32)
+        if ny == 2:
+            return own + self.plane_in[turn * ny + 1, q % 2].astype(F32)
+        terms = [own] + [self.plane_in[turn * ny + o, q % 2].astype(F32) for o in range(1, ny)]
+        total = jnp.zeros_like(own)
+        for y in range(ny):
+            offset = lax.rem(place.y - y + ny, ny)
+            for o in range(ny):
+                total = total + jnp.where(offset == o, terms[o], 0.0)
+        return total
+
+    def plane_mid(self):
+        for o in range(self.ny):
+            self.planes[(0, o)].wait_recv()
+        for q in range(4):
+            self.plane_out[1, q] = self.plane_sum(0, q).astype(BF)
+        self.plane_send(1)
+
+    def plane_end(self):
+        for o in range(self.ny):
+            self.planes[(1, o)].wait_recv()
+        for q in range(4):
+            self.total[q] = self.plane_sum(1, q)
+
+    def deliver(self, targets):
+        place = self.place
+        base = 4 + self.n + 2 * self.ny
+        self.outs = []
+        for i, (q, count, target) in enumerate(targets):
+            source = self.total.at[q] if count is None else self.total.at[pl.ds(q, count)]
+            copy = remote(source, target, self.send.at[base + i], self.recv.at[base + i], place.at(dk=1))
+            self.copies.append(copy)
+            self.outs.append(copy)
+            own = pltpu.make_async_copy(source, target, self.local.at[i])
+            own.start()
+            self.owns.append(own)
+
+    def finish(self):
+        for copy in self.outs:
+            copy.wait_recv()
+
+    def drain(self):
+        for copy in self.copies:
+            copy.wait_send()
+        for copy in self.owns:
+            copy.wait()
+
+
+class SmallReduce:
+    def __init__(self, place, total, landing, send, recv):
+        self.place, self.total, self.landing, self.send, self.recv = place, total, landing, send, recv
+        n, ny = place.n, place.ny
+        self.stages = [
+            [place.at(dk=1)],
+            [place.at(dz=o) for o in range(1, n)],
+            [place.at(dr=1)],
+            [place.at(dy=o) for o in range(1, ny)],
+        ]
+        self.copies = []
+        self.slot = 0
+
+    @staticmethod
+    def count(n, ny):
+        return 1 + (n - 1) + 1 + (ny - 1)
+
+    def start(self, stage):
+        self.current = []
+        for device in self.stages[stage]:
+            slot = self.slot
+            copy = remote(
+                self.total.at[stage], self.landing.at[slot], self.send.at[slot], self.recv.at[slot], device
+            )
+            self.current.append((slot, copy))
+            self.copies.append(copy)
+            self.slot += 1
+
+    def end(self, stage):
+        place, ny = self.place, self.place.ny
+        for _, copy in self.current:
+            copy.wait_recv()
+        terms = [self.total[stage]] + [self.landing[slot] for slot, _ in self.current]
+        if stage == 3 and ny > 2:
+            total = jnp.zeros_like(terms[0])
+            for y in range(ny):
+                offset = lax.rem(place.y - y + ny, ny)
+                for o in range(ny):
+                    total = total + jnp.where(offset == o, terms[o], 0.0)
+        else:
+            total = functools.reduce(lambda a, b: a + b, terms)
+        self.total[stage + 1] = total
+
+    def steps(self):
+        out = [functools.partial(self.start, 0)]
+        for stage in range(4):
+            out.append(functools.partial(self.end, stage))
+            if stage < 3:
+                out.append(functools.partial(self.start, stage + 1))
+        return out
+
+
+SLOTS = 3
+
+
+def reduce_kernel(n, ny, *refs):
+    grads, small = refs[:6], refs[6]
+    out_qkv, out_ao, out_in, out_out, out_small = refs[7:12]
+    bufs = refs[12:]
+    slots = [bufs[3 * s : 3 * s + 3] for s in range(SLOTS)]
+    bufs = bufs[3 * SLOTS :]
+    landings = [bufs[3 * g : 3 * g + 3] for g in range(6)]
+    small_total, small_landing, local, send, recv, small_send, small_recv = bufs[18:]
+    place = Place(n, ny)
+    half = D // n // 2
+    mine = pl.ds(pl.multiple_of(place.k * half, half), half)
+    small_total[0] = small[...]
+    order = [5, 4, 3, 2, 1, 0]
+    groups = {}
+    for i, g in enumerate(order):
+        groups[g] = Reduce(
+            place, g % 3 == 2, slots[i % SLOTS], landings[g], local.at[g], send.at[g], recv.at[g]
+        )
+    place.greet(place.everyone())
+    for g in order:
+        groups[g].core(grads[g])
+
+    def targets(g):
+        b, kind = g // 3, g % 3
+        if kind == 0:
+            return [(0, 3, out_qkv.at[b, :, mine]), (3, None, out_ao.at[b, mine])]
+        if kind == 1:
+            return [(q, None, out_in.at[b, mine, pl.ds(q * D, D)]) for q in range(4)]
+        return [(0, 4, out_out.at[b, :, mine])]
+
+    def begin(i):
+        if i >= SLOTS:
+            groups[order[i - SLOTS]].drain()
+        groups[order[i]].load(grads[order[i]])
+
+    def end(g):
+        groups[g].plane_end()
+        groups[g].deliver(targets(g))
+
+    def steps(i):
+        g = order[i]
+        group = groups[g]
+        out = [functools.partial(begin, i), group.add_cores]
+        out += [functools.partial(group.ring_step, d) for d in range(n // 2 - 1, 0, -1)]
+        out += [group.ring_end, group.plane_mid, functools.partial(end, g)]
+        return out
+
+    small_sum = SmallReduce(place, small_total, small_landing, small_send, small_recv)
+    plans = [steps(i) for i in range(6)]
+    length = len(plans[0])
+    gap = max(1, -(-(length + 1) // SLOTS))
+    small_steps = small_sum.steps()
+    for t in range(length + gap * 5):
+        for i in range(6):
+            at = t - gap * i
+            if 0 <= at < length:
+                plans[i][at]()
+        if small_steps:
+            small_steps.pop(0)()
+    while small_steps:
+        small_steps.pop(0)()
+    out_small[...] = small_total[4]
+    for i, g in enumerate(order):
+        groups[g].finish()
+        if i >= 6 - SLOTS:
+            groups[g].drain()
+    for copy in small_sum.copies:
+        copy.wait_send()
+
+
+def reduce_grads(n, ny, grads, small):
+    rows = D // n
+    out = [
+        jax.ShapeDtypeStruct((2, 3, rows, D), F32),
+        jax.ShapeDtypeStruct((2, rows, D), F32),
+        jax.ShapeDtypeStruct((2, rows, 4 * D), F32),
+        jax.ShapeDtypeStruct((2, 4, rows, D), F32),
+        jax.ShapeDtypeStruct(small.shape, F32),
+    ]
+    anywhere = pl.BlockSpec(memory_space=pl.ANY)
+    vmem = pl.BlockSpec(memory_space=pltpu.VMEM)
+    scratch = []
+    for s in range(SLOTS):
+        scratch += Reduce.slot_buffers(n)
+    for g in range(6):
+        scratch += Reduce.landing_buffers(n, ny)
+    smalls = SmallReduce.count(n, ny)
+    scratch += [
+        pltpu.VMEM((5,) + small.shape, F32),
+        pltpu.VMEM((smalls,) + small.shape, F32),
+        pltpu.SemaphoreType.DMA((6, 8)),
+        pltpu.SemaphoreType.DMA((6, Reduce.count(n, ny))),
+        pltpu.SemaphoreType.DMA((6, Reduce.count(n, ny))),
+        pltpu.SemaphoreType.DMA((smalls,)),
+        pltpu.SemaphoreType.DMA((smalls,)),
+    ]
+    return pl.pallas_call(
+        functools.partial(reduce_kernel, n, ny),
+        out_shape=out,
+        in_specs=[anywhere] * 6 + [vmem],
+        out_specs=[anywhere] * 4 + [vmem],
+        scratch_shapes=scratch,
+        compiler_params=pltpu.CompilerParams(
+            collective_id=1, has_side_effects=True, vmem_limit_bytes=60 * MIB
+        ),
+        name="reduce_grads",
+    )(*grads, small)
 
 
 def layer_norm(operand, scale_row, shift_row):
@@ -133,7 +706,8 @@
     mixed = mixed_sum.astype(jnp.bfloat16)
     first_sum = inputs + matmul(mixed, out_mat) + bias_rows[1].astype(jnp.float32)
     normed = layer_norm(first_sum, gains_f[0], shifts_f[0])
-    hidden = matmul(normed.astype(jnp.bfloat16), in_mat) + ffn_bias.astype(jnp.float32)
+    hidden = jnp.concatenate([matmul(normed.astype(jnp.bfloat16), in_mat[q]) for q in range(4)], axis=1)
+    hidden = hidden + ffn_bias.astype(jnp.float32)
     active = jax.nn.gelu(hidden, approximate=False).astype(jnp.bfloat16)
     second_sum = normed + matmul(active, down_mat) + bias_rows[2].astype(jnp.float32)
     output = layer_norm(second_sum, gains_f[1], shifts_f[1])
@@ -184,9 +758,12 @@
         lambda pre_act: jax.nn.gelu(pre_act, approximate=False), hidden
     )
     grad_hidden = pull_gelu(grad_active)[0].astype(jnp.bfloat16)
-    grad_in = matmul_left_t(normed.astype(jnp.bfloat16), grad_hidden)
+    normed_bf = normed.astype(jnp.bfloat16)
+    grad_in = jnp.stack([matmul_left_t(normed_bf, grad_hidden[:, q * D : q * D + D]) for q in range(4)])
     grad_ffn_bias = jnp.sum(grad_hidden.astype(jnp.float32), axis=0)
-    grad_normed = grad_second + matmul_right_t(grad_hidden, in_mat)
+    grad_normed = grad_second + sum(
+        matmul_right_t(grad_hidden[:, q * D : q * D + D], in_mat[q]) for q in range(4)
+    )
     unused_first, pull_first = jax.vjp(layer_norm, first_sum, gains_f[0], shifts_f[0])
     grad_first, grad_gain_one, grad_shift_one = pull_first(grad_normed)
     grad_branch = grad_first.astype(jnp.bfloat16)
@@ -223,17 +800,25 @@
         + matmul_right_t(grad_key, qkv_mats[1])
         + matmul_right_t(grad_value, qkv_mats[2])
     )
-    grads_block = (
-        grad_qkv,
-        grad_out_mat,
-        grad_in,
-        grad_down,
-        grad_query_bias,
-        jnp.stack([grad_bias_value, grad_bias_two, grad_bias_three], axis=0),
-        grad_ffn_bias,
-        jnp.stack([grad_gain_one, grad_gain_two], axis=0),
-        jnp.stack([grad_shift_one, grad_shift_two], axis=0),
-    )
+    mats = (
+        jnp.concatenate([grad_qkv, grad_out_mat[None]], axis=0).astype(jnp.bfloat16),
+        grad_in.astype(jnp.bfloat16),
+        grad_down.astype(jnp.bfloat16),
+    )
+    rows = jnp.stack(
+        [
+            grad_query_bias,
+            grad_bias_value,
+            grad_bias_two,
+            grad_bias_three,
+            grad_gain_one,
+            grad_gain_two,
+            grad_shift_one,
+            grad_shift_two,
+        ]
+    )
+    small = jnp.concatenate([rows, grad_ffn_bias.reshape(4, D)], axis=0)
+    grads_block = (mats, small)
     return (grad_inputs, grads_block)
 
 
@@ -250,100 +835,81 @@
     bias_ff,
     norm_gain,
     norm_shift,
+    n,
+    ny,
 ):
     length = lengths[0]
     row_count = tokens.shape[1]
+    width = D // n
     first_row = lax.axis_index("ctx") * row_count
     valid_rows = (first_row + jnp.arange(row_count) < length).astype(jnp.float32)
+    small = jnp.concatenate(
+        [
+            bias_q,
+            bias_d.reshape(6, width),
+            norm_gain.reshape(4, width),
+            norm_shift.reshape(4, width),
+            bias_ff.reshape(8, width),
+            jnp.zeros((8, width), BF),
+        ],
+        axis=0,
+    )
+    gathered = gather_weights(
+        n, ny, w_qkv, w_attn_out, w_in, w_out.reshape(2, 4, width, D), small
+    )
+    fulls, small_full = gathered[:6], gathered[6]
+    narrow = small_full[:, :16].transpose(1, 0, 2).reshape(16, D)
+    ff = small_full[:, 16:24].reshape(n, 2, 4 * width).transpose(1, 0, 2).reshape(2, 4 * D)
+    weights = []
+    for b in range(2):
+        first = fulls[3 * b].reshape(4, D, D)
+        weights.append(
+            (
+                first[:3],
+                first[3],
+                fulls[3 * b + 1].reshape(4, D, D),
+                fulls[3 * b + 2].reshape(4 * D, D),
+                narrow[b],
+                narrow[2 + 3 * b : 5 + 3 * b],
+                ff[b],
+                narrow[8 + 2 * b : 10 + 2 * b],
+                narrow[12 + 2 * b : 14 + 2 * b],
+            )
+        )
     carried = tokens[0].astype(jnp.float32)
-    kept_weights = []
     kept_layers = []
     for layer_idx in range(2):
-        weights_full = (
-            lax.all_gather(w_qkv[layer_idx], "fsdp", axis=1, tiled=True),
-            lax.all_gather(w_attn_out[layer_idx], "fsdp", axis=0, tiled=True),
-            lax.all_gather(w_in[layer_idx], "fsdp", axis=0, tiled=True),
-            lax.all_gather(w_out[layer_idx], "fsdp", axis=0, tiled=True),
-            lax.all_gather(bias_q[layer_idx], "fsdp", axis=0, tiled=True),
-            lax.all_gather(bias_d[layer_idx], "fsdp", axis=1, tiled=True),
-            lax.all_gather(bias_ff[layer_idx], "fsdp", axis=0, tiled=True),
-            lax.all_gather(norm_gain[layer_idx], "fsdp", axis=1, tiled=True),
-            lax.all_gather(norm_shift[layer_idx], "fsdp", axis=1, tiled=True),
-        )
-        kept_weights.append(weights_full)
-        carried, kept_acts = block_forward(carried, weights_full, length)
+        carried, kept_acts = block_forward(carried, weights[layer_idx], length)
         kept_layers.append(kept_acts)
     output_tokens = carried.astype(jnp.bfloat16)[None]
     grad_carried = cotangent[0].astype(jnp.float32) * valid_rows[:, None]
-    reduced = [None, None]
+    grads = [None] * 6
+    smalls = [None, None]
     for layer_idx in (1, 0):
-        weights_full = (
-            lax.all_gather(w_qkv[layer_idx], "fsdp", axis=1, tiled=True),
-            lax.all_gather(w_attn_out[layer_idx], "fsdp", axis=0, tiled=True),
-            lax.all_gather(w_in[layer_idx], "fsdp", axis=0, tiled=True),
-            lax.all_gather(w_out[layer_idx], "fsdp", axis=0, tiled=True),
-            lax.all_gather(bias_q[layer_idx], "fsdp", axis=0, tiled=True),
-            lax.all_gather(bias_d[layer_idx], "fsdp", axis=1, tiled=True),
-            lax.all_gather(bias_ff[layer_idx], "fsdp", axis=0, tiled=True),
-            lax.all_gather(norm_gain[layer_idx], "fsdp", axis=1, tiled=True),
-            lax.all_gather(norm_shift[layer_idx], "fsdp", axis=1, tiled=True),
+        grad_carried, (mats, smalls[layer_idx]) = block_backward(
+            grad_carried, weights[layer_idx], kept_layers[layer_idx]
         )
-        grad_carried, grads_block = block_backward(
-            grad_carried, weights_full, kept_layers[layer_idx]
-        )
-        shard_sums = (
-            lax.psum_scatter(
-                grads_block[0].astype(jnp.bfloat16), "fsdp", scatter_dimension=1, tiled=True
-            ).astype(jnp.float32),
-            lax.psum_scatter(
-                grads_block[1].astype(jnp.bfloat16), "fsdp", scatter_dimension=0, tiled=True
-            ).astype(jnp.float32),
-            lax.psum_scatter(
-                grads_block[2].astype(jnp.bfloat16), "fsdp", scatter_dimension=0, tiled=True
-            ).astype(jnp.float32),
-            lax.psum_scatter(
-                grads_block[3].astype(jnp.bfloat16), "fsdp", scatter_dimension=0, tiled=True
-            ).astype(jnp.float32),
-            lax.psum_scatter(
-                grads_block[4].astype(jnp.bfloat16), "fsdp", scatter_dimension=0, tiled=True
-            ).astype(jnp.float32),
-            lax.psum_scatter(
-                grads_block[5].astype(jnp.bfloat16), "fsdp", scatter_dimension=1, tiled=True
-            ).astype(jnp.float32),
-            lax.psum_scatter(
-                grads_block[6].astype(jnp.bfloat16), "fsdp", scatter_dimension=0, tiled=True
-            ).astype(jnp.float32),
-            lax.psum_scatter(
-                grads_block[7].astype(jnp.bfloat16), "fsdp", scatter_dimension=1, tiled=True
-            ).astype(jnp.float32),
-            lax.psum_scatter(
-                grads_block[8].astype(jnp.bfloat16), "fsdp", scatter_dimension=1, tiled=True
-            ).astype(jnp.float32),
-        )
-        reduced[layer_idx] = (
-            lax.psum(shard_sums[0].astype(jnp.bfloat16), ("rep", "ctx")).astype(jnp.float32),
-            lax.psum(shard_sums[1].astype(jnp.bfloat16), ("rep", "ctx")).astype(jnp.float32),
-            lax.psum(shard_sums[2].astype(jnp.bfloat16), ("rep", "ctx")).astype(jnp.float32),
-            lax.psum(shard_sums[3].astype(jnp.bfloat16), ("rep", "ctx")).astype(jnp.float32),
-            lax.psum(shard_sums[4].astype(jnp.bfloat16), ("rep", "ctx")).astype(jnp.float32),
-            lax.psum(shard_sums[5].astype(jnp.bfloat16), ("rep", "ctx")).astype(jnp.float32),
-            lax.psum(shard_sums[6].astype(jnp.bfloat16), ("rep", "ctx")).astype(jnp.float32),
-            lax.psum(shard_sums[7].astype(jnp.bfloat16), ("rep", "ctx")).astype(jnp.float32),
-            lax.psum(shard_sums[8].astype(jnp.bfloat16), ("rep", "ctx")).astype(jnp.float32),
-        )
-    stacked = [jnp.stack([reduced[0][member], reduced[1][member]], axis=0) for member in range(9)]
+        grads[3 * layer_idx] = mats[0].reshape(4, n, width, D)
+        grads[3 * layer_idx + 1] = mats[1].reshape(4, n, width, D)
+        grads[3 * layer_idx + 2] = mats[2].reshape(n, 4, width, D)
+    small_grads = jnp.concatenate(smalls, axis=0)
+    out_qkv, out_ao, out_in, out_out, small_sum = reduce_grads(n, ny, grads, small_grads)
+    z = lax.axis_index("fsdp")
+    small_sum = small_sum.reshape(2, 12, D)
+    own = lax.dynamic_slice_in_dim(small_sum, z * width, width, 2)
+    own_ff = lax.dynamic_slice_in_dim(small_sum[:, 8:].reshape(2, 4 * D), z * 4 * width, 4 * width, 1)
     return (
         output_tokens,
         grad_carried[None],
-        stacked[0],
-        stacked[1],
-        stacked[2],
-        stacked[3],
-        stacked[4],
-        stacked[5],
-        stacked[6],
-        stacked[7],
-        stacked[8],
+        out_qkv,
+        out_ao,
+        out_in,
+        out_out.reshape(2, 4 * width, D),
+        own[:, 0],
+        own[:, 1:4],
+        own_ff,
+        own[:, 4:6],
+        own[:, 6:8],
     )
 
 
@@ -362,8 +928,9 @@
         P(None, None, "fsdp"),
         P(None, None, "fsdp"),
     )
+    n, ny = mesh.shape["fsdp"], mesh.shape["ctx"] // 2
     return jax.shard_map(
-        body,
+        functools.partial(body, n=n, ny=ny),
         mesh=mesh,
         in_specs=placed,
         out_specs=(

time: 1770 us -> 1070 us (0.60)
  waiting for transfers between devices: 1140 us -> 109 us
  Pallas kernels: 0 us -> 546 us
  blocking collectives: 171 us -> 0 us
  matrix products: 152 us -> 126 us
    pallas_call x0 -> x2, Pallas kernels: none -> 546 us  [the longest x1 297 us: reduce_grads(): pl.pallas_call(functools.partial(reduce_kernel, n, ny), out_shape=out, in...]
    reduce_scatter x6 -> x0, waiting for transfers between devices: 409 us -> none  [the longest x2 176 us: body(): lax.psum_scatter(grads_block[3].astype(jnp.bfloat16), 'fsdp', scatter_dim...]
    all_gather x8 -> x0, waiting for transfers between devices: 360 us -> none  [the longest x2 155 us: body(): lax.all_gather(w_out[layer_idx], 'fsdp', axis=0, tiled=True)]
    unnamed x39 -> x8, waiting for transfers between devices: 180 us -> 0.64 us
    all_gather x8 -> x0, blocking collectives: 122 us -> none  [the longest x2 33.2 us: body(): lax.all_gather(norm_shift[layer_idx], 'fsdp', axis=1, tiled=True)]
    psum x1 -> x0, waiting for transfers between devices: 97.4 us -> none  [body(): lax.psum(shard_sums[0].astype(jnp.bfloat16), ('rep', 'ctx'))]
    unnamed x181 -> x278, local copies, waits for them, and re-layouts: 66 us -> 29.1 us
    dot_general x12 -> x18, matrix products: 50 us -> 20.7 us  [matmul(): return jnp.dot(operand_a, operand_b, preferred_element_type=jnp.float32)]
  transfers between devices with their start and end apart: 31 -> 8, of which waited for: 24 -> 7; matrix products, arithmetic and copies ran while one was open for 14% -> 8% of each run, Pallas kernels for 0% -> 0%
where the time goes in v1:
time: 1070 us; the launch traced here: 1060 us
  Pallas kernels  546 us (51%)
  local copies, waits for them, and re-layouts  184 us (17%)
  matrix products  126 us (12%)
  waiting for transfers between devices  109 us (10%)
  other arithmetic  61.8 us (6%)
  loops' own time  17 us (2%)
  between operations  16.7 us (2%)
    pallas_call x1, Pallas kernels, reduce_grads(): pl.pallas_call(functools.partial(reduce_kernel, n, ny), out_shape=out, in...  297 us
    pallas_call x1, Pallas kernels, gather_weights(): pl.pallas_call(functools.partial(gather_kernel, n, ny), out_shape=out, in...  249 us
    dynamic_slice x84, local copies, waits for them, and re-layouts, head_slices(): lax.dynamic_slice_in_dim(matrix, group_idx * (2 * HEAD), 2 * HEAD, 1)  68.2 us
    dot_general x18, matrix products, matmul_left_t(): lax.dot_general(operand_a, operand_b, (((0,), (0,)), ((), ())), preferred...  33.3 us
    reduce_scatter x2, waiting for transfers between devices, block_backward(): lax.psum_scatter(grad_key_all.astype(jnp.bfloat16), 'ctx', scatter_dimens...  29.6 us
    unnamed x278, local copies, waits for them, and re-layouts  29.1 us
    dot_general x18, matrix products, matmul_right_t(): lax.dot_general(operand_a, operand_b, (((1,), (1,)), ((), ())), preferred...  28.9 us
    all_gather x2, waiting for transfers between devices, block_forward(): lax.all_gather(key_rows, 'ctx', axis=0, tiled=True)  28.4 us
  transfers between devices with their start and end apart: 8, of which 7 were waited for; matrix products, arithmetic and copies ran while one was open for 8% of the time, Pallas kernels for 0%

profile of v1, /device:TPU:0, one launch (start us, length us, event | category | flops | bytes accessed | tf_op | source)
XLA Modules:
  0.0 1061.8 jit_solution(5177217436155703847)
XLA Ops:
  10.1 3.1 concatenate.36.refs_4_
  13.2 249.3 %gather_weights.1 = (bf16[4,4,192,768]{3,2,1,0:T(8,128)(2,1)}, bf16[4,4,192,768]{3,2,1,0:T(8,128)(2,1)}, bf16[4,4,192,768]{3,2,1,0:T(8,128)(2,1)}, bf16[4,4,192,...) custom-call(bf16[2,3,192,768]{3,2,1,0:T(8,128)(2,1)} %refs_0_.1, ...), custom_call_target="tpu_custom_call" | custom-call | tf_op jit(solution)/shard_map/gather_weights/pallas_call | solution.py:218
  264.0 6.6 fusion.108
  277.7 2.6 fusion.49
  280.3 7.0 fusion.106
  287.3 3.0 all-gather.5.cloned.1.call-done
  290.3 22.0 %all-gather.7.cloned.1.call-done = bf16[1024,768]{0,1:T(8,128)(2,1)} async-done(((bf16[256,768]{0,1:T(8,128)(2,1)}), bf16[1024,768]{0,1:T(8,128)(2,1)}) %all-gather.7.cloned.1.call-update) | async-done | bytes 1572880 | tf_op jit(solution)/shard_map/all_gather | solution.py:701
  312.4 34.3 %while.56 = (s32[]{:T(128)}, bf16[6,256,128]{1,2,0:T(8,128)(2,1)S(1)}, f32[6,2,256]{2,1,0:T(2,128)S(1)}, s32[6]{0:T(128)S(1)}, bf16[1024,768]{0,1:T(8,128)(2,1)}...) while((s32[]{:T(128)}, ...), condition=%wide.region_3.4_spmd.clone, body=%wide.region_0.3_spmd.clone.sunk | while | flops 140509696 | bytes 8278211 | solution.py:640
  350.9 7.7 multiply_convert_fusion.3
  376.4 6.4 all-gather.11.cloned.1.call-done
  382.8 2.6 copy.38
  385.4 19.1 %all-gather.9.cloned.1.call-done = bf16[1024,768]{1,0:T(8,128)(2,1)} async-done(((bf16[256,768]{1,0:T(8,128)(2,1)}), bf16[1024,768]{1,0:T(8,128)(2,1)}) %all-gather.9.cloned.1.call-update) | async-done | bytes 1572880 | tf_op jit(solution)/shard_map/all_gather | solution.py:702
  404.5 2.6 copy.36
  407.9 38.0 %while.57 = (s32[]{:T(128)}, bf16[6,256,128]{1,2,0:T(8,128)(2,1)}, f32[6,2,256]{2,1,0:T(2,128)S(1)}, s32[6]{0:T(128)S(1)}, bf16[1024,768]{0,1:T(8,128)(2,1)}, /*...) while((s32[]{:T(128)}, bf16[6,256,128]{1,2,0:T(8,128)(2,1)}, ...), condition=%wide.region_11.12_spmd.clone, body=%wide.region_8.11_spmd.clone.sunk | while | flops 140509696 | bytes 8278719 | solution.py:640
  450.7 6.8 multiply_convert_fusion.2
  462.4 3.5 convert_reduce_fusion
  474.0 59.1 %while.58 = (s32[]{:T(128)}, bf16[6,256,128]{1,2,0:T(8,128)(2,1)S(1)}, bf16[6,1024,128]{1,2,0:T(8,128)(2,1)}, bf16[6,1024,128]{1,2,0:T(8,128)(2,1)}, s32[6]{0:T(...) while((s32[]{:T(128)}, ...), condition=%wide.region_22.23_spmd.clone, body=%wide.region_20.22_spmd.clone.sunk | while | flops 340591104 | bytes 20001508 | solution.py:681
  540.3 2.8 fusion.36
  545.6 16.0 %reduce-scatter.5.cloned.1.call-done = bf16[256,768]{0,1:T(8,128)(2,1)} async-done(((bf16[1024,768]{0,1:T(8,128)(2,1)}), bf16[256,768]{0,1:T(8,128)(2,1)}) %reduce-scatter.5.cloned.1.call-update) | async-done | bytes 393232 | tf_op jit(solution)/shard_map/reduce_scatter | solution.py:777
  561.6 2.7 convolution_add_fusion.7
  564.3 28.1 %reduce-scatter.7.cloned.1.call-done = bf16[256,768]{0,1:T(8,128)(2,1)} async-done(((bf16[1024,768]{0,1:T(8,128)(2,1)}), bf16[256,768]{0,1:T(8,128)(2,1)}) %reduce-scatter.7.cloned.1.call-update) | async-done | bytes 393232 | tf_op jit(solution)/shard_map/reduce_scatter | solution.py:780
  592.4 3.1 multiply_reduce_fusion.3
  597.5 5.1 convert_reduce_fusion.1
  613.0 58.9 %while.59 = (s32[]{:T(128)}, bf16[6,256,128]{1,2,0:T(8,128)(2,1)S(1)}, bf16[6,1024,128]{1,2,0:T(8,128)(2,1)}, bf16[6,1024,128]{1,2,0:T(8,128)(2,1)}, s32[6]{0:T(...) while((s32[]{:T(128)}, ...), condition=%wide.region_31.32_spmd.clone, body=%wide.region_29.31_spmd.clone.sunk | while | flops 340591104 | bytes 20001508 | solution.py:681
  672.0 2.6 fusion.35
  678.3 3.6 convolution_convert_fusion
  681.9 2.7 pad_maximum_fusion.3.refs_4_
  694.2 2.6 convolution_convert_fusion.11
  704.2 3.7 convolution_convert_fusion.1
  707.9 2.8 pad_maximum_fusion.2.refs_3_
  718.2 13.6 %reduce-scatter.9.cloned.1.call-done = bf16[256,768]{0,1:T(8,128)(2,1)} async-done(((bf16[1024,768]{0,1:T(8,128)(2,1)}), bf16[256,768]{0,1:T(8,128)(2,1)}) %reduce-scatter.9.cloned.1.call-update) | async-done | bytes 393232 | tf_op jit(solution)/shard_map/reduce_scatter | solution.py:777
  738.1 297.1 %reduce_grads.1 = (f32[2,3,192,768]{3,2,1,0:T(8,128)}, f32[2,192,768]{2,1,0:T(8,128)}, f32[2,192,3072]{2,1,0:T(8,128)}, f32[2,4,192,768]{3,2,1,0:T(8,128)}, f32[24,768]{1,0:T(8,128)}) custom-call(bf16[4,4,192,768]{3,2,1,0:T(8,128)(2,1)} %pad_maximum_fusion.refs_0_, bf16[4,4,192,768]{3,2,1,0:T(8,128)(2,1)} %pad_maximum_fusion.1.refs_1_, ...), custom_call_target="tpu_custom_call" | custom-call | tf_op jit(solution)/shard_map/reduce_grads/pallas_call | solution.py:575
  (747 shorter events, 299.4 us)
Async XLA Ops:
  7.2 283.1 %all-gather.5.cloned.1.call-start = ((), (), s32[]{:S(2)}) async-start(), calls=%async_computation.4 | async-start | bytes 1966080 | tf_op jit(solution)/shard_map/all_gather | solution.py:702
  270.6 76.1 %copy-start = (bf16[1,4,192,768]{3,2,1,0:T(8,128)(2,1)}, bf16[1,4,192,768]{3,2,1,0:T(8,128)(2,1)S(1)}, u32[]{:S(2)}) copy-start(bf16[1,4,192,768]{3,2,1,0:T(8,128)(2,1)S(1)} %get-tuple-element.606) | copy-start | bytes 3538948
  272.2 40.1 %all-gather.7.cloned.1.call-start = ((), (), s32[]{:S(2)}) async-start(), calls=%async_computation.5 | async-start | bytes 1966080 | tf_op jit(solution)/shard_map/all_gather | solution.py:701
  274.8 108.0 %all-gather.11.cloned.1.call-start = ((), (), s32[]{:S(2)}) async-start(), calls=%async_computation.7 | async-start | bytes 1966080 | tf_op jit(solution)/shard_map/all_gather | solution.py:701
  277.0 84.1 %copy-start.75 = (f32[768]{0:T(1024)}, f32[768]{0:T(1024)S(1)}, u32[]{:S(2)}) copy-start(f32[768]{0:T(1024)S(1)} %add.321) | copy-start | bytes 9220
  277.7 73.2 %copy-start.69 = (f32[1,4,768]{2,0,1:T(1,128)}, f32[1,4,768]{2,0,1:T(1,128)S(1)}, u32[]{:S(2)}) copy-start(f32[1,4,768]{2,0,1:T(1,128)S(1)} %get-tuple-element.586) | copy-start | bytes 36868
  347.3 11.3 %copy-start.79 = (f32[256]{0:T(256)}, f32[256]{0:T(256)S(1)}, u32[]{:S(2)}) copy-start(f32[256]{0:T(256)S(1)} %broadcast_multiply_fusion.3) | copy-start | bytes 3076
  347.6 11.1 %copy-start.85 = (f32[256]{0:T(256)}, f32[256]{0:T(256)S(1)}, u32[]{:S(2)}) copy-start(f32[256]{0:T(256)S(1)} %fusion.96) | copy-start | bytes 3076
  350.0 8.7 copy-start.57
  350.4 8.3 slice-start.4
  350.9 7.8 copy-start.59
  361.7 12.0 %copy-start.29 = (bf16[256,768]{1,0:T(8,128)(2,1)}, bf16[256,768]{1,0:T(8,128)(2,1)S(1)}, u32[]{:S(2)}) copy-start(bf16[256,768]{1,0:T(8,128)(2,1)S(1)} %fusion.59) | copy-start | bytes 1179652
  363.0 41.5 %all-gather.9.cloned.1.call-start = ((), (), s32[]{:S(2)}) async-start(), calls=%async_computation.6 | async-start | bytes 1966080 | tf_op jit(solution)/shard_map/all_gather | solution.py:702
  366.3 195.3 %reduce-scatter.5.cloned.1.call-start = ((), (), s32[]{:S(2)}) async-start(), calls=%async_computation.8 | async-start | bytes 1966080 | tf_op jit(solution)/shard_map/reduce_scatter | solution.py:777
  407.8 38.0 %copy-start.37 = (bf16[1,4,192,768]{3,2,1,0:T(8,128)(2,1)S(1)}, bf16[1,4,192,768]{3,2,1,0:T(8,128)(2,1)}, u32[]{:S(2)}) copy-start(bf16[1,4,192,768]{3,2,1,0:T(8,128)(2,1)} %get-tuple-element.602) | copy-start | bytes 3538948
  407.8 38.0 %copy-start.76 = (f32[768]{0:T(1024)S(1)}, f32[768]{0:T(1024)}, u32[]{:S(2)}) copy-start(f32[768]{0:T(1024)} %copy-done.75) | copy-start | bytes 9220
  407.8 38.0 %copy-start.82 = (f32[256]{0:T(256)S(1)}, f32[256]{0:T(256)}, u32[]{:S(2)}) copy-start(f32[256]{0:T(256)} %copy-done.81) | copy-start | bytes 3076
  407.9 38.0 %copy-start.123 = (f32[768]{0:T(1024)S(1)}, f32[768]{0:T(1024)}, u32[]{:S(2)}) copy-start(f32[768]{0:T(1024)} %reshape.606) | copy-start | bytes 9220
  449.4 8.2 slice-start.6
  533.3 59.0 %reduce-scatter.7.cloned.1.call-start = ((), (), s32[]{:S(2)}) async-start(), calls=%async_computation.9 | async-start | bytes 1966080 | tf_op jit(solution)/shard_map/reduce_scatter | solution.py:780
  533.9 180.4 %reduce-scatter.11.cloned.1.call-start = ((), (), s32[]{:S(2)}) async-start(), calls=%async_computation.11 | async-start | bytes 1966080 | tf_op jit(solution)/shard_map/reduce_scatter | solution.py:780
  540.2 21.3 %copy-start.9 = (bf16[1,4,192,768]{3,2,1,0:T(8,128)(2,1)S(1)}, bf16[1,4,192,768]{3,2,1,0:T(8,128)(2,1)}, u32[]{:S(2)}) copy-start(bf16[1,4,192,768]{3,2,1,0:T(8,128)(2,1)} %get-tuple-element.601) | copy-start | bytes 3538948
  545.6 46.8 %copy-start.84 = (f32[256]{0:T(256)S(1)}, f32[256]{0:T(256)}, u32[]{:S(2)}) copy-start(f32[256]{0:T(256)} %copy-done.81) | copy-start | bytes 3076
  564.3 31.2 %copy-start.118 = (f32[256]{0:T(256)S(1)}, f32[256]{0:T(256)}, u32[]{:S(2)}) copy-start(f32[256]{0:T(256)} %copy-done.117) | copy-start | bytes 3076
  613.0 59.0 %copy-start.26 = (bf16[6,256,128]{1,2,0:T(8,128)(2,1)S(1)}, bf16[6,256,128]{1,2,0:T(8,128)(2,1)}, u32[]{:S(2)}) copy-start(bf16[6,256,128]{1,2,0:T(8,128)(2,1)} %copy-done.24) | copy-start | bytes 1179652
  671.9 59.8 %reduce-scatter.9.cloned.1.call-start = ((), (), s32[]{:S(2)}) async-start(), calls=%async_computation.10 | async-start | bytes 1966080 | tf_op jit(solution)/shard_map/reduce_scatter | solution.py:777
  714.3 19.0 %copy-start.40 = (bf16[1,4,192,768]{3,2,1,0:T(8,128)(2,1)S(1)}, bf16[1,4,192,768]{3,2,1,0:T(8,128)(2,1)}, u32[]{:S(2)}) copy-start(bf16[1,4,192,768]{3,2,1,0:T(8,128)(2,1)} %fusion.34) | copy-start | bytes 3538948
  714.3 19.0 %copy-start.41 = (bf16[768,768]{0,1:T(8,128)(2,1)S(1)}, bf16[768,768]{0,1:T(8,128)(2,1)}, u32[]{:S(2)}) copy-start(bf16[768,768]{0,1:T(8,128)(2,1)} %convolution_convert_fusion.17) | copy-start | bytes 3538948
  738.1 304.5 %copy-start.33 = (bf16[1,4,192,768]{3,2,1,0:T(8,128)(2,1)S(1)}, bf16[1,4,192,768]{3,2,1,0:T(8,128)(2,1)}, u32[]{:S(2)}) copy-start(bf16[1,4,192,768]{3,2,1,0:T(8,128)(2,1)} %get-tuple-element.605) | copy-start | bytes 3538948
  738.1 304.5 %copy-start.61 = (f32[256,768]{1,0:T(8,128)S(1)}, f32[256,768]{1,0:T(8,128)}, u32[]{:S(2)}) copy-start(f32[256,768]{1,0:T(8,128)} %convolution_add_fusion.2) | copy-start | bytes 2359300
  1035.1 9.1 copy-start.32
  1035.2 9.1 copy-start.48
  (108 other events, 320.5 us)
Sparse Core Ops, SparseCore 0:
  272.3 17.9 all-gather.4
  292.4 19.8 all-gather.6
  363.1 19.6 all-gather.10
  384.8 19.6 all-gather.8
  533.4 28.1 reduce-scatter.4
  564.1 28.1 reduce-scatter.6
  672.0 28.1 reduce-scatter.10
  703.5 28.1 reduce-scatter.8

commit v2 on v1

--- a/solution.py
+++ b/solution.py
@@ -25,31 +25,43 @@
         self.n, self.ny = n, ny
         self.r = lax.axis_index("rep")
         self.z = lax.axis_index("fsdp")
-        c = lax.axis_index("ctx")
-        self.y, self.k = lax.div(c, 2), lax.rem(c, 2)
-        self.p = lax.rem(self.r + self.y, 2)
+        self.c = lax.axis_index("ctx")
+        self.y, self.k = lax.div(self.c, 2), lax.rem(self.c, 2)
+        self.e = lax.rem(self.y, 2)
+        self.q = 2 * self.e + self.r
+        self.qx = 2 * self.e + (1 - self.r)
+        self.qy = 2 * (1 - self.e) + self.r
+        self.qd = 2 * (1 - self.e) + (1 - self.r)
 
     def shard(self, offset):
         return lax.rem(self.z + (offset + self.n), self.n)
 
-    def at(self, dr=0, dz=0, dy=0, dk=0):
-        r = lax.rem(self.r + dr, 2)
-        y = lax.rem(self.y + (dy + self.ny), self.ny)
-        k = lax.rem(self.k + dk, 2)
-        return (r, self.shard(dz), 2 * y + k)
-
-    def greet(self, others):
+    def up(self, offset):
+        return (self.r, self.shard(offset), self.c)
+
+    def x(self):
+        return (1 - self.r, self.z, self.c)
+
+    def across(self):
+        return (self.r, self.z, 2 * (self.y + 1 - 2 * self.e) + self.k)
+
+    def row(self, offset, flip=0):
+        y = lax.rem(self.y + offset, self.ny)
+        k = self.k + flip * (1 - 2 * self.k)
+        return (self.r, self.z, 2 * y + k)
+
+    def core(self):
+        return self.row(0, 1)
+
+    def greet(self):
+        others = [self.up(o) for o in range(1, self.n)]
+        others += [self.x(), self.core()]
+        others += [self.row(o) for o in range(1, self.ny)]
         barrier = pltpu.get_barrier_semaphore()
         for other in others:
             pl.semaphore_signal(barrier, inc=1, device_id=other, device_id_type=MESH)
         pl.semaphore_wait(barrier, len(others))
 
-    def everyone(self):
-        others = [self.at(dz=o) for o in range(1, self.n)]
-        others += [self.at(dr=1), self.at(dk=1)]
-        others += [self.at(dy=o) for o in range(1, self.ny)]
-        return others
-
 
 def remote(src, dst, send, recv, device):
     copy = pltpu.make_async_remote_copy(
@@ -57,6 +69,11 @@
     )
     copy.start()
     return copy
+
+
+def halves(half):
+    first = -(-half // 32) * 16
+    return [(0, first), (first, half - first)]
 
 
 class Gather:
@@ -65,23 +82,22 @@
         self.local, self.send, self.recv = local, send, recv
         self.n = place.n
         self.half = full.shape[2] // 2
-        self.copies = []
-        self.core_copies = []
+        self.pieces = halves(self.half)
+        self.copies, self.core_copies = [], []
 
     @staticmethod
     def count(n):
-        return 6 * n - 4
-
-    def part(self, shard, q0, count, k):
-        rows = pl.ds(pl.multiple_of(k * self.half, self.half), self.half)
-        if self.by_shard:
-            return self.full.at[shard, pl.ds(q0, count), rows]
-        return self.full.at[pl.ds(q0, count), shard, rows]
+        return 10 * (n - 1)
+
+    def part(self, shard, q, piece=None):
+        start, size = (0, self.half) if piece is None else piece
+        rows = pl.ds(pl.multiple_of(self.place.k * self.half + start, 8), size)
+        return self.full.at[shard, q, rows] if self.by_shard else self.full.at[q, shard, rows]
 
     def load(self, sources):
         self.loads = []
+        z = self.place.z
         for i, (q, count, source) in enumerate(sources):
-            z = self.place.z
             if self.by_shard:
                 target = self.full.at[z]
             elif count is None:
@@ -92,83 +108,64 @@
             copy.start()
             self.loads.append(copy)
 
-    def share(self, piece, slot, device, core=False):
+    def share(self, kind, offset, piece, device):
+        slot = kind * (self.n - 1) + offset - 1
         copy = remote(piece, piece, self.send.at[slot], self.recv.at[slot], device)
-        (self.core_copies if core else self.copies).append(copy)
+        self.copies.append(copy)
         return copy
 
-    def core_share(self, shard, q0, count, slot):
+    def core_share(self, kind, offset, piece):
+        copy = self.share(5 + kind, offset, piece, self.place.core())
+        self.core_copies.append(copy)
+
+    def start(self):
         place = self.place
-        base = self.n + 2 * (self.n - 1)
-        self.share(self.part(shard, q0, count, place.k), base + slot, place.at(dk=1), core=True)
-
-    def start(self):
-        place, n = self.place, self.n
         for copy in self.loads:
             copy.wait()
-        self.plus, self.minus = {}, {}
-        self.xs, self.ys = {}, {}
-        mine = self.part(place.z, 2 * place.p, 2, place.k)
-        if n // 2 > 1:
-            self.plus[1] = self.share(mine, 0, place.at(dz=1))
-            self.minus[1] = self.share(mine, n // 2, place.at(dz=-1))
-        else:
-            self.plus[1] = self.share(self.part(place.z, 2 * place.p, 1, place.k), 0, place.at(dz=1))
-            self.minus[1] = self.share(self.part(place.z, 2 * place.p + 1, 1, place.k), 1, place.at(dz=-1))
-
-    def hop(self, d, forward):
-        place, n = self.place, self.n
-        sign = 1 if forward else -1
-        table = self.plus if forward else self.minus
-        table[d].wait_recv()
-        shard = place.shard(-sign * d)
-        q0 = 2 * place.p + (0 if forward else 1)
-        base = 0 if forward else n // 2
-        if d < n // 2:
-            if d + 1 < n // 2:
-                piece = self.part(shard, 2 * place.p, 2, place.k)
-            else:
-                piece = self.part(shard, q0, 1, place.k)
-            table[d + 1] = self.share(piece, base + d, place.at(dz=sign))
-        whole = d < n // 2
-        distance = (sign * d) % n
-        if whole or forward:
-            slot = n + distance - 1
-            self.xs[distance] = self.share(self.part(shard, 2 * place.p, 1, place.k), slot, place.at(dr=1))
-        if whole or not forward:
-            slot = n + (n - 1) + distance - 1
-            self.ys[distance] = self.share(self.part(shard, 2 * place.p + 1, 1, place.k), slot, place.at(dy=1))
-        if whole:
-            self.core_share(shard, 2 * place.p, 2, base + d - 1)
-        else:
-            self.core_share(shard, q0, 1, base + d - 1)
-
-    def hops(self, d):
-        self.hop(d, True)
-        self.hop(d, False)
-
-    def cross(self, which):
-        place, n = self.place, self.n
-        table = (self.xs, self.ys)[which]
-        for distance in sorted(table, key=lambda o: min(o, n - o)):
-            table[distance].wait_recv()
-            shard = place.shard(-distance)
-            q = 2 * (1 - place.p) + which
-            self.core_share(shard, q, 1, n + which * (n - 1) + distance - 1)
+        mine = self.part(place.z, place.q)
+        self.ups = [self.share(0, o, mine, place.up(o)) for o in range(1, self.n)]
+
+    def plane(self):
+        place = self.place
+        self.xs, self.ys = [], []
+        for o in range(1, self.n):
+            self.ups[o - 1].wait_recv()
+            piece = self.part(place.shard(-o), place.q)
+            self.xs.append(self.share(1, o, piece, place.x()))
+            self.ys.append(self.share(2, o, piece, place.across()))
+            self.core_share(0, o, piece)
+
+    def diagonal(self):
+        place = self.place
+        self.dys, self.dxs = [], []
+        for o in range(1, self.n):
+            shard = place.shard(-o)
+            self.xs[o - 1].wait_recv()
+            self.dys.append(self.share(3, o, self.part(shard, place.qx, self.pieces[0]), place.across()))
+            self.core_share(1, o, self.part(shard, place.qx))
+            self.ys[o - 1].wait_recv()
+            self.dxs.append(self.share(4, o, self.part(shard, place.qy, self.pieces[1]), place.x()))
+            self.core_share(2, o, self.part(shard, place.qy))
+
+    def last(self):
+        place = self.place
+        for o in range(1, self.n):
+            shard = place.shard(-o)
+            self.dys[o - 1].wait_recv()
+            self.core_share(3, o, self.part(shard, place.qd, self.pieces[0]))
+            self.dxs[o - 1].wait_recv()
+            self.core_share(4, o, self.part(shard, place.qd, self.pieces[1]))
 
     def finish(self):
         for copy in self.core_copies:
             copy.wait_recv()
 
     def drain(self):
-        for copy in self.core_copies + self.copies:
+        for copy in self.copies:
             copy.wait_send()
 
     def steps(self):
-        out = [self.start]
-        out += [functools.partial(self.hops, d) for d in range(1, self.n // 2 + 1)]
-        out += [functools.partial(self.cross, 0), functools.partial(self.cross, 1), self.finish]
-        return out
+        return [self.start, self.plane, self.diagonal, self.last, self.finish]
 
 
 def weight_sources(b, qkv, ao, win, wout):
@@ -181,8 +178,9 @@
 
 def gather_kernel(n, ny, *refs):
     qkv, ao, win, wout, small = refs[:5]
-    fulls, small_full = refs[5:11], refs[11]
-    local, send, recv, small_send, small_recv = refs[12:]
+    outs, small_full = refs[5:11], refs[11]
+    fulls = refs[12:18]
+    local, send, recv, small_send, small_recv = refs[18:]
     place = Place(n, ny)
     groups = []
     for g in range(6):
@@ -192,18 +190,25 @@
         groups.append(group)
     own = pltpu.make_async_copy(small, small_full.at[place.z], small_send.at[0])
     own.start()
-    place.greet(place.everyone())
+    place.greet()
     smalls = [
-        remote(small, small_full.at[place.z], small_send.at[o], small_recv.at[o], place.at(dz=o))
+        remote(small, small_full.at[place.z], small_send.at[o], small_recv.at[o], place.up(o))
         for o in range(1, n)
     ]
     steps = [group.steps() for group in groups]
+    kept = []
     for t in range(len(steps[0]) + 5):
         for g in range(6):
             if 0 <= t - g < len(steps[g]):
                 steps[g][t - g]()
+                if t - g == len(steps[g]) - 1:
+                    copy = pltpu.make_async_copy(fulls[g], outs[g], local.at[g, 4])
+                    copy.start()
+                    kept.append(copy)
     for group in groups:
         group.drain()
+    for copy in kept:
+        copy.wait()
     own.wait()
     for copy in smalls:
         copy.wait()
@@ -220,46 +225,60 @@
         out_shape=out,
         in_specs=[anywhere] * 5,
         out_specs=[anywhere] * 7,
-        scratch_shapes=[
-            pltpu.SemaphoreType.DMA((6, 4)),
+        scratch_shapes=[pltpu.VMEM(shape, BF) for shape in shapes]
+        + [
+            pltpu.SemaphoreType.DMA((6, 5)),
             pltpu.SemaphoreType.DMA((6, Gather.count(n))),
             pltpu.SemaphoreType.DMA((6, Gather.count(n))),
             pltpu.SemaphoreType.DMA((n,)),
             pltpu.SemaphoreType.DMA((n,)),
         ],
-        compiler_params=pltpu.CompilerParams(collective_id=0, has_side_effects=True),
+        compiler_params=pltpu.CompilerParams(
+            collective_id=0, has_side_effects=True, vmem_limit_bytes=40 * MIB
+        ),
         name="gather_weights",
     )(qkv, ao, win, wout, small)
 
 
 class Reduce:
-    def __init__(self, place, by_shard, slot, landing, local, send, recv):
-        self.place, self.by_shard = place, by_shard
-        self.half_in, self.plane_out, self.total = slot
-        self.core_in, self.ring_in, self.plane_in = landing
+    def __init__(self, place, by_shard, slot, landing, out, local, send, recv):
+        self.place, self.by_shard, self.out = place, by_shard, out
+        (self.half_in,) = slot
+        self.core_in, self.x_in, self.y_in, self.dx_in, self.dy_in, self.z_in, self.far_in = landing
         self.local, self.send, self.recv = local, send, recv
         self.n, self.ny = place.n, place.ny
         self.half = self.half_in.shape[2]
+        self.pieces = halves(self.half)
         self.copies, self.owns = [], []
-        self.rings, self.planes = {}, {}
+        self.slot = 0
 
     @staticmethod
     def count(n, ny):
-        return 4 + n + 2 * ny + 4
+        return 4 + 6 + (n - 1) + (ny // 2 - 1) + 9
 
     @staticmethod
     def slot_buffers(n):
-        half = D // n // 2
-        return [pltpu.VMEM((n, 4, half, D), BF), pltpu.VMEM((2, 4, half, D), BF), pltpu.VMEM((4, half, D), F32)]
+        return [pltpu.VMEM((n, 4, D // n // 2, D), BF)]
 
     @staticmethod
     def landing_buffers(n, ny):
         half = D // n // 2
+        (_, first), (_, second) = halves(half)
         return [
             pltpu.VMEM((n, 4, half, D), BF),
-            pltpu.VMEM((2, n // 2, 4, half, D), BF),
-            pltpu.VMEM((2 * ny, 2, half, D), BF),
+            pltpu.VMEM((n, half, D), BF),
+            pltpu.VMEM((n, half, D), BF),
+            pltpu.VMEM((n, first, D), BF),
+            pltpu.VMEM((n, second, D), BF),
+            pltpu.VMEM((n - 1, half, D), BF),
+            pltpu.VMEM((max(1, ny // 2 - 1), half, D), BF),
         ]
+
+    def share(self, src, dst, device):
+        copy = remote(src, dst, self.send.at[self.slot], self.recv.at[self.slot], device)
+        self.slot += 1
+        self.copies.append(copy)
+        return copy
 
     def parts_of(self, grad, k):
         rows = pl.ds(pl.multiple_of(k * self.half, self.half), self.half)
@@ -270,41 +289,21 @@
     def load(self, grad):
         self.loaded = []
         for i, (q, part) in enumerate(self.parts_of(grad, self.place.k)):
-            copy = pltpu.make_async_copy(part, self.half_in.at[:, q], self.local.at[4 + i])
+            copy = pltpu.make_async_copy(part, self.half_in.at[:, q], self.local.at[i])
             copy.start()
             self.loaded.append(copy)
 
     def core(self, grad):
-        self.cored = []
-        for i, (q, part) in enumerate(self.parts_of(grad, 1 - self.place.k)):
-            copy = remote(
-                part, self.core_in.at[:, q], self.send.at[i], self.recv.at[i], self.place.at(dk=1)
-            )
-            self.cored.append(copy)
-            self.copies.append(copy)
-
-    def ring_send(self, d):
-        place, n = self.place, self.n
-        for sign in (1, -1):
-            way = 0 if sign == 1 else 1
-            shard = place.shard(sign * d)
-            if d == n // 2:
-                q0, count = 2 * way, 2
-            else:
-                q0, count = 0, 4
-            slot = 4 + way * (n // 2) + d - 1
-            copy = remote(
-                self.half_in.at[shard, pl.ds(q0, count)],
-                self.ring_in.at[way, d - 1, pl.ds(q0, count)],
-                self.send.at[slot],
-                self.recv.at[slot],
-                place.at(dz=sign),
-            )
-            self.rings[(way, d)] = copy
-            self.copies.append(copy)
-
-    def add_into(self, target, source):
-        target[...] = (target[...].astype(F32) + source[...].astype(F32)).astype(BF)
+        self.cored = [
+            self.share(part, self.core_in.at[:, q], self.place.core())
+            for q, part in self.parts_of(grad, 1 - self.place.k)
+        ]
+
+    def add_into(self, target, *sources):
+        total = target[...].astype(F32)
+        for source in sources:
+            total = total + source[...].astype(F32)
+        target[...] = total.astype(BF)
 
     def add_cores(self):
         for copy in self.loaded:
@@ -318,100 +317,104 @@
             return 0
 
         lax.fori_loop(0, 4 * self.n, one, 0)
-        self.ring_send(self.n // 2)
-
-    def ring_step(self, d):
-        place, n = self.place, self.n
-        for sign in (1, -1):
-            way = 0 if sign == 1 else 1
-            self.rings[(way, d + 1)].wait_recv()
-            shard = place.shard(sign * d)
-            qs = range(4) if d + 1 < n // 2 else range(2 * way, 2 * way + 2)
-            for q in qs:
-                self.add_into(self.half_in.at[shard, q], self.ring_in.at[way, d, q])
-        self.ring_send(d)
-
-    def ring_end(self):
         place = self.place
-        for way in (0, 1):
-            self.rings[(way, 1)].wait_recv()
-        for q in range(4):
-            total = self.half_in[place.z, q].astype(F32)
-            for way in (0, 1):
-                if self.n > 2 or q // 2 == way:
-                    total = total + self.ring_in[way, 0, q].astype(F32)
-            self.plane_out[0, q] = total.astype(BF)
-        self.plane_send(0)
-
-    def plane_send(self, turn):
-        place, ny = self.place, self.ny
-        base = 4 + self.n + turn * ny
-        slot = base
-        qx = 2 * turn
-        copy = remote(
-            self.plane_out.at[turn, pl.ds(qx, 2)],
-            self.plane_in.at[turn * ny],
-            self.send.at[slot],
-            self.recv.at[slot],
-            place.at(dr=1),
-        )
-        self.planes[(turn, 0)] = copy
-        self.copies.append(copy)
-        for o in range(1, ny):
-            copy = remote(
-                self.plane_out.at[turn, pl.ds(2 - qx, 2)],
-                self.plane_in.at[turn * ny + o],
-                self.send.at[slot + o],
-                self.recv.at[slot + o],
-                place.at(dy=o),
-            )
-            self.planes[(turn, o)] = copy
-            self.copies.append(copy)
-
-    def plane_sum(self, turn, q):
-        place, ny = self.place, self.ny
-        over_x = (q // 2 == 0) == (turn == 0)
-        own = self.plane_out[turn, q].astype(F32)
-        if over_x:
-            return own + self.plane_in[turn * ny, q % 2].astype(F32)
-        if ny == 2:
-            return own + self.plane_in[turn * ny + 1, q % 2].astype(F32)
-        terms = [own] + [self.plane_in[turn * ny + o, q % 2].astype(F32) for o in range(1, ny)]
-        total = jnp.zeros_like(own)
-        for y in range(ny):
-            offset = lax.rem(place.y - y + ny, ny)
-            for o in range(ny):
-                total = total + jnp.where(offset == o, terms[o], 0.0)
-        return total
-
-    def plane_mid(self):
-        for o in range(self.ny):
-            self.planes[(0, o)].wait_recv()
-        for q in range(4):
-            self.plane_out[1, q] = self.plane_sum(0, q).astype(BF)
-        self.plane_send(1)
-
-    def plane_end(self):
-        for o in range(self.ny):
-            self.planes[(1, o)].wait_recv()
-        for q in range(4):
-            self.total[q] = self.plane_sum(1, q)
-
-    def deliver(self, targets):
+        (a, first), (b, second) = self.pieces
+        top, low = pl.ds(a, first), pl.ds(b, second)
+        self.dx = self.share(self.half_in.at[:, place.qd, top], self.dx_in, place.x())
+        self.dy = self.share(self.half_in.at[:, place.qd, low], self.dy_in, place.across())
+        self.planes = [
+            self.share(self.half_in.at[:, place.qx, top], self.x_in.at[:, top], place.x()),
+            self.share(self.half_in.at[:, place.qy, low], self.y_in.at[:, low], place.across()),
+        ]
+
+    def plane(self):
         place = self.place
-        base = 4 + self.n + 2 * self.ny
-        self.outs = []
-        for i, (q, count, target) in enumerate(targets):
-            source = self.total.at[q] if count is None else self.total.at[pl.ds(q, count)]
-            copy = remote(source, target, self.send.at[base + i], self.recv.at[base + i], place.at(dk=1))
-            self.copies.append(copy)
-            self.outs.append(copy)
-            own = pltpu.make_async_copy(source, target, self.local.at[i])
-            own.start()
-            self.owns.append(own)
+        (a, first), (b, second) = self.pieces
+        top, low = pl.ds(a, first), pl.ds(b, second)
+        self.dx.wait_recv()
+
+        def one(j, _):
+            self.add_into(self.half_in.at[j, place.qy, top], self.dx_in.at[j])
+            return 0
+
+        lax.fori_loop(0, self.n, one, 0)
+        self.planes.append(self.share(self.half_in.at[:, place.qy, top], self.y_in.at[:, top], place.across()))
+        self.dy.wait_recv()
+
+        def two(j, _):
+            self.add_into(self.half_in.at[j, place.qx, low], self.dy_in.at[j])
+            return 0
+
+        lax.fori_loop(0, self.n, two, 0)
+        self.planes.append(self.share(self.half_in.at[:, place.qx, low], self.x_in.at[:, low], place.x()))
+
+    def depth(self):
+        place = self.place
+        for copy in self.planes:
+            copy.wait_recv()
+
+        def one(j, _):
+            self.add_into(self.half_in.at[j, place.q], self.x_in.at[j], self.y_in.at[j])
+            return 0
+
+        lax.fori_loop(0, self.n, one, 0)
+        self.deep = [
+            self.share(self.half_in.at[place.shard(o), place.q], self.z_in.at[o - 1], place.up(o))
+            for o in range(1, self.n)
+        ]
+
+    def mine(self, q, piece=None):
+        start, size = (0, self.half) if piece is None else piece
+        return self.out.at[q, pl.ds(pl.multiple_of(self.place.k * self.half + start, 8), size)]
+
+    def total(self):
+        place = self.place
+        for copy in self.deep:
+            copy.wait_recv()
+        own = self.half_in.at[place.z, place.q]
+        self.add_into(own, *[self.z_in.at[o - 1] for o in range(1, self.n)])
+        if self.ny > 2:
+            far = [self.share(own, self.far_in.at[i], place.row(2 * i + 2)) for i in range(self.ny // 2 - 1)]
+            for copy in far:
+                copy.wait_recv()
+            mine = own[...].astype(F32)
+            terms = [mine] + [self.far_in[i].astype(F32) for i in range(self.ny // 2 - 1)]
+            total = jnp.zeros_like(mine)
+            for y in range(0, self.ny, 2):
+                offset = lax.rem(place.y - place.e - y + self.ny, self.ny)
+                for i, term in enumerate(terms):
+                    total = total + jnp.where(offset == 2 * i, term, 0.0)
+            own[...] = total.astype(BF)
+        copy = pltpu.make_async_copy(own, self.mine(place.q), self.local.at[4])
+        copy.start()
+        self.owns.append(copy)
+        self.spread = [
+            self.share(own, self.mine(place.q), place.x()),
+            self.share(own, self.mine(place.q), place.across()),
+        ]
+        self.cores = [self.share(own, self.mine(place.q), place.core())]
+
+    def forward(self, q, device, piece=None):
+        return self.share(self.mine(q, piece), self.mine(q, piece), device)
+
+    def turn(self):
+        place = self.place
+        self.spread[0].wait_recv()
+        self.dy = self.forward(place.qx, place.across(), self.pieces[0])
+        self.cores.append(self.forward(place.qx, place.core()))
+        self.spread[1].wait_recv()
+        self.dx = self.forward(place.qy, place.x(), self.pieces[1])
+        self.cores.append(self.forward(place.qy, place.core()))
+
+    def last(self):
+        place = self.place
+        self.dy.wait_recv()
+        self.cores.append(self.forward(place.qd, place.core(), self.pieces[0]))
+        self.dx.wait_recv()
+        self.cores.append(self.forward(place.qd, place.core(), self.pieces[1]))
 
     def finish(self):
-        for copy in self.outs:
+        for copy in self.cores:
             copy.wait_recv()
 
     def drain(self):
@@ -420,16 +423,19 @@
         for copy in self.owns:
             copy.wait()
 
+    def steps(self):
+        return [self.add_cores, self.plane, self.depth, self.total, self.turn, self.last]
+
 
 class SmallReduce:
     def __init__(self, place, total, landing, send, recv):
         self.place, self.total, self.landing, self.send, self.recv = place, total, landing, send, recv
         n, ny = place.n, place.ny
         self.stages = [
-            [place.at(dk=1)],
-            [place.at(dz=o) for o in range(1, n)],
-            [place.at(dr=1)],
-            [place.at(dy=o) for o in range(1, ny)],
+            [place.core()],
+            [place.up(o) for o in range(1, n)],
+            [place.x()],
+            [place.row(o) for o in range(1, ny)],
         ]
         self.copies = []
         self.slot = 0
@@ -473,60 +479,38 @@
         return out
 
 
-SLOTS = 3
+SLOTS = 4
 
 
 def reduce_kernel(n, ny, *refs):
     grads, small = refs[:6], refs[6]
-    out_qkv, out_ao, out_in, out_out, out_small = refs[7:12]
-    bufs = refs[12:]
-    slots = [bufs[3 * s : 3 * s + 3] for s in range(SLOTS)]
-    bufs = bufs[3 * SLOTS :]
-    landings = [bufs[3 * g : 3 * g + 3] for g in range(6)]
-    small_total, small_landing, local, send, recv, small_send, small_recv = bufs[18:]
+    outs, out_small = refs[7:13], refs[13]
+    bufs = refs[14:]
+    slots = [bufs[s : s + 1] for s in range(SLOTS)]
+    bufs = bufs[SLOTS:]
+    landings = [bufs[7 * g : 7 * g + 7] for g in range(6)]
+    small_total, small_landing, local, send, recv, small_send, small_recv = bufs[42:]
     place = Place(n, ny)
-    half = D // n // 2
-    mine = pl.ds(pl.multiple_of(place.k * half, half), half)
     small_total[0] = small[...]
     order = [5, 4, 3, 2, 1, 0]
     groups = {}
     for i, g in enumerate(order):
         groups[g] = Reduce(
-            place, g % 3 == 2, slots[i % SLOTS], landings[g], local.at[g], send.at[g], recv.at[g]
+            place, g % 3 == 2, slots[i % SLOTS], landings[g], outs[g], local.at[g], send.at[g], recv.at[g]
         )
-    place.greet(place.everyone())
+    place.greet()
     for g in order:
         groups[g].core(grads[g])
-
-    def targets(g):
-        b, kind = g // 3, g % 3
-        if kind == 0:
-            return [(0, 3, out_qkv.at[b, :, mine]), (3, None, out_ao.at[b, mine])]
-        if kind == 1:
-            return [(q, None, out_in.at[b, mine, pl.ds(q * D, D)]) for q in range(4)]
-        return [(0, 4, out_out.at[b, :, mine])]
 
     def begin(i):
         if i >= SLOTS:
             groups[order[i - SLOTS]].drain()
         groups[order[i]].load(grads[order[i]])
 
-    def end(g):
-        groups[g].plane_end()
-        groups[g].deliver(targets(g))
-
-    def steps(i):
-        g = order[i]
-        group = groups[g]
-        out = [functools.partial(begin, i), group.add_cores]
-        out += [functools.partial(group.ring_step, d) for d in range(n // 2 - 1, 0, -1)]
-        out += [group.ring_end, group.plane_mid, functools.partial(end, g)]
-        return out
-
     small_sum = SmallReduce(place, small_total, small_landing, small_send, small_recv)
-    plans = [steps(i) for i in range(6)]
+    plans = [[functools.partial(begin, i)] + groups[order[i]].steps() for i in range(6)]
     length = len(plans[0])
-    gap = max(1, -(-(length + 1) // SLOTS))
+    gap = max(1, -(-length // SLOTS))
     small_steps = small_sum.steps()
     for t in range(length + gap * 5):
         for i in range(6):
@@ -548,13 +532,7 @@
 
 def reduce_grads(n, ny, grads, small):
     rows = D // n
-    out = [
-        jax.ShapeDtypeStruct((2, 3, rows, D), F32),
-        jax.ShapeDtypeStruct((2, rows, D), F32),
-        jax.ShapeDtypeStruct((2, rows, 4 * D), F32),
-        jax.ShapeDtypeStruct((2, 4, rows, D), F32),
-        jax.ShapeDtypeStruct(small.shape, F32),
-    ]
+    out = [jax.ShapeDtypeStruct((4, rows, D), BF)] * 6 + [jax.ShapeDtypeStruct(small.shape, F32)]
     anywhere = pl.BlockSpec(memory_space=pl.ANY)
     vmem = pl.BlockSpec(memory_space=pltpu.VMEM)
     scratch = []
@@ -566,7 +544,7 @@
     scratch += [
         pltpu.VMEM((5,) + small.shape, F32),
         pltpu.VMEM((smalls,) + small.shape, F32),
-        pltpu.SemaphoreType.DMA((6, 8)),
+        pltpu.SemaphoreType.DMA((6, 5)),
         pltpu.SemaphoreType.DMA((6, Reduce.count(n, ny))),
         pltpu.SemaphoreType.DMA((6, Reduce.count(n, ny))),
         pltpu.SemaphoreType.DMA((smalls,)),
@@ -576,7 +554,7 @@
         functools.partial(reduce_kernel, n, ny),
         out_shape=out,
         in_specs=[anywhere] * 6 + [vmem],
-        out_specs=[anywhere] * 4 + [vmem],
+        out_specs=[anywhere] * 6 + [vmem],
         scratch_shapes=scratch,
         compiler_params=pltpu.CompilerParams(
             collective_id=1, has_side_effects=True, vmem_limit_bytes=60 * MIB
@@ -893,7 +871,7 @@
         grads[3 * layer_idx + 1] = mats[1].reshape(4, n, width, D)
         grads[3 * layer_idx + 2] = mats[2].reshape(n, 4, width, D)
     small_grads = jnp.concatenate(smalls, axis=0)
-    out_qkv, out_ao, out_in, out_out, small_sum = reduce_grads(n, ny, grads, small_grads)
+    *sums, small_sum = reduce_grads(n, ny, grads, small_grads)
     z = lax.axis_index("fsdp")
     small_sum = small_sum.reshape(2, 12, D)
     own = lax.dynamic_slice_in_dim(small_sum, z * width, width, 2)
@@ -901,10 +879,10 @@
     return (
         output_tokens,
         grad_carried[None],
-        out_qkv,
-        out_ao,
-        out_in,
-        out_out.reshape(2, 4 * width, D),
+        jnp.stack([sums[0][:3], sums[3][:3]]).astype(F32),
+        jnp.stack([sums[0][3], sums[3][3]]).astype(F32),
+        jnp.stack([sums[1], sums[4]]).transpose(0, 2, 1, 3).reshape(2, width, 4 * D).astype(F32),
+        jnp.stack([sums[2], sums[5]]).reshape(2, 4 * width, D).astype(F32),
         own[:, 0],
         own[:, 1:4],
         own_ff,

time: 1070 us -> 829 us (0.77)
  Pallas kernels: 546 us -> 286 us
  waiting for transfers between devices: 109 us -> 121 us
    pallas_call x1, Pallas kernels: 249 us -> 110 us  [gather_weights(): pl.pallas_call(functools.partial(gather_kernel, n, ny), out_shape=out, in...]
    pallas_call x1, Pallas kernels: 297 us -> 176 us  [reduce_grads(): pl.pallas_call(functools.partial(reduce_kernel, n, ny), out_shape=out, in...]
    unnamed x278 -> x270, local copies, waits for them, and re-layouts: 29.1 us -> 28.6 us
  transfers between devices with their start and end apart: 8 -> 8, of which waited for: 7 -> 7; matrix products, arithmetic and copies ran while one was open for 8% -> 10% of each run, Pallas kernels for 0% -> 0%
where the time goes in v2:
time: 829 us; the launch traced here: 820 us
  Pallas kernels  286 us (34%)
  local copies, waits for them, and re-layouts  187 us (23%)
  waiting for transfers between devices  121 us (15%)
  matrix products  120 us (14%)
  other arithmetic  70.9 us (9%)
  loops' own time  17 us (2%)
  between operations  16.9 us (2%)
    pallas_call x1, Pallas kernels, reduce_grads(): pl.pallas_call(functools.partial(reduce_kernel, n, ny), out_shape=out, in...  176 us
    pallas_call x1, Pallas kernels, gather_weights(): pl.pallas_call(functools.partial(gather_kernel, n, ny), out_shape=out, in...  110 us
    dynamic_slice x84, local copies, waits for them, and re-layouts, head_slices(): lax.dynamic_slice_in_dim(matrix, group_idx * (2 * HEAD), 2 * HEAD, 1)  62.7 us
    reduce_scatter x2, waiting for transfers between devices, block_backward(): lax.psum_scatter(grad_key_all.astype(jnp.bfloat16), 'ctx', scatter_dimens...  33.2 us
    all_gather x2, waiting for transfers between devices, block_forward(): lax.all_gather(value_rows, 'ctx', axis=0, tiled=True)  30.4 us
    unnamed x270, local copies, waits for them, and re-layouts  28.6 us
    all_gather x2, waiting for transfers between devices, block_forward(): lax.all_gather(key_rows, 'ctx', axis=0, tiled=True)  28.4 us
    dot_general x18, matrix products, matmul_left_t(): lax.dot_general(operand_a, operand_b, (((0,), (0,)), ((), ())), preferred...  28.2 us
  transfers between devices with their start and end apart: 8, of which 7 were waited for; matrix products, arithmetic and copies ran while one was open for 10% of the time, Pallas kernels for 0%

profile of v2, /device:TPU:0, one launch (start us, length us, event | category | flops | bytes accessed | tf_op | source)
XLA Modules:
  0.0 819.6 jit_solution(4137214666186224307)
XLA Ops:
  16.7 109.6 %gather_weights.1 = (bf16[4,4,192,768]{3,2,1,0:T(8,128)(2,1)S(1)}, bf16[4,4,192,768]{3,2,1,0:T(8,128)(2,1)}, bf16[4,4,192,768]{3,2,1,0:T(8,128)(2,1)}, bf16[4,4,...) custom-call(bf16[2,3,192,768]{3,2,1,0:T(8,128)(2,1)S(1)} %copy-done., ...), custom_call_target="tpu_custom_call" | custom-call | tf_op jit(solution)/shard_map/gather_weights/pallas_call | solution.py:223
  129.2 6.4 fusion.108
  146.5 7.0 fusion.106
  153.5 10.4 %all-gather.5.cloned.1.call-done = bf16[1024,768]{0,1:T(8,128)(2,1)} async-done(((bf16[256,768]{0,1:T(8,128)(2,1)}), bf16[1024,768]{0,1:T(8,128)(2,1)}) %all-gather.5.cloned.1.call-update) | async-done | bytes 1572880 | tf_op jit(solution)/shard_map/all_gather | solution.py:680
  164.0 22.0 %all-gather.7.cloned.1.call-done = bf16[1024,768]{0,1:T(8,128)(2,1)} async-done(((bf16[256,768]{0,1:T(8,128)(2,1)}), bf16[1024,768]{0,1:T(8,128)(2,1)}) %all-gather.7.cloned.1.call-update) | async-done | bytes 1572880 | tf_op jit(solution)/shard_map/all_gather | solution.py:679
  186.1 34.4 %while.56 = (s32[]{:T(128)}, bf16[6,256,128]{1,2,0:T(8,128)(2,1)S(1)}, f32[6,2,256]{2,1,0:T(2,128)S(1)}, s32[6]{0:T(128)S(1)}, bf16[1024,768]{0,1:T(8,128)(2,1)}...) while((s32[]{:T(128)}, ...), condition=%wide.region_3.4_spmd.clone, body=%wide.region_0.3_spmd.clone.sunk | while | flops 140509696 | bytes 8278211 | solution.py:618
  226.0 7.7 multiply_convert_fusion.3
  251.4 6.4 all-gather.11.cloned.1.call-done
  259.5 20.0 %all-gather.9.cloned.1.call-done = bf16[1024,768]{1,0:T(8,128)(2,1)} async-done(((bf16[256,768]{1,0:T(8,128)(2,1)}), bf16[1024,768]{1,0:T(8,128)(2,1)}) %all-gather.9.cloned.1.call-update) | async-done | bytes 1572880 | tf_op jit(solution)/shard_map/all_gather | solution.py:680
  279.5 2.6 copy.36
  284.0 45.0 %while.57 = (s32[]{:T(128)}, bf16[6,256,128]{1,2,0:T(8,128)(2,1)}, f32[6,2,256]{2,1,0:T(2,128)}, s32[6]{0:T(128)}, bf16[1024,768]{0,1:T(8,128)(2,1)}, /*index=5*...) while((s32[]{:T(128)}, bf16[6,256,128]{1,2,0:T(8,128)(2,1)}, ...), condition=%wide.region_11.12_spmd.clone, body=%wide.region_8.11_spmd.clone.sunk | while | flops 140509696 | bytes 8279227 | solution.py:618
  328.9 2.6 fusion.112
  334.7 6.8 multiply_convert_fusion.2
  345.2 3.1 convert_reduce_fusion
  355.1 54.0 %while.58 = (s32[]{:T(128)}, bf16[6,256,128]{1,2,0:T(8,128)(2,1)S(1)}, bf16[6,1024,128]{1,2,0:T(8,128)(2,1)}, bf16[6,1024,128]{1,2,0:T(8,128)(2,1)}, s32[6]{0:T(...) while((s32[]{:T(128)}, ...), condition=%wide.region_22.23_spmd.clone, body=%wide.region_20.22_spmd.clone.sunk | while | flops 340591104 | bytes 20001508 | solution.py:659
  415.8 2.8 fusion.36
  418.7 2.5 convolution_add_fusion.8
  421.2 16.3 %reduce-scatter.5.cloned.1.call-done = bf16[256,768]{0,1:T(8,128)(2,1)} async-done(((bf16[1024,768]{0,1:T(8,128)(2,1)}), bf16[256,768]{0,1:T(8,128)(2,1)}) %reduce-scatter.5.cloned.1.call-update) | async-done | bytes 393232 | tf_op jit(solution)/shard_map/reduce_scatter | solution.py:755
  437.5 2.7 convolution_add_fusion.7
  440.2 28.1 %reduce-scatter.7.cloned.1.call-done = bf16[256,768]{0,1:T(8,128)(2,1)} async-done(((bf16[1024,768]{0,1:T(8,128)(2,1)}), bf16[256,768]{0,1:T(8,128)(2,1)}) %reduce-scatter.7.cloned.1.call-update) | async-done | bytes 393232 | tf_op jit(solution)/shard_map/reduce_scatter | solution.py:758
  468.3 3.1 multiply_reduce_fusion.3
  473.3 5.1 convert_reduce_fusion.1
  488.8 58.9 %while.59 = (s32[]{:T(128)}, bf16[6,256,128]{1,2,0:T(8,128)(2,1)S(1)}, bf16[6,1024,128]{1,2,0:T(8,128)(2,1)}, bf16[6,1024,128]{1,2,0:T(8,128)(2,1)}, s32[6]{0:T(...) while((s32[]{:T(128)}, ...), condition=%wide.region_31.32_spmd.clone, body=%wide.region_29.31_spmd.clone.sunk | while | flops 340591104 | bytes 20001508 | solution.py:659
  553.1 3.6 convolution_convert_fusion
  570.4 2.7 fusion.34
  576.9 3.7 convolution_convert_fusion.1
  580.6 2.7 pad_maximum_fusion.2.refs_3_
  588.1 2.5 convolution_convert_fusion.15
  590.6 16.9 %reduce-scatter.9.cloned.1.call-done = bf16[256,768]{0,1:T(8,128)(2,1)} async-done(((bf16[1024,768]{0,1:T(8,128)(2,1)}), bf16[256,768]{0,1:T(8,128)(2,1)}) %reduce-scatter.9.cloned.1.call-update) | async-done | bytes 393232 | tf_op jit(solution)/shard_map/reduce_scatter | solution.py:755
  613.9 176.1 %reduce_grads.1 = (bf16[4,192,768]{2,1,0:T(8,128)(2,1)}, bf16[4,192,768]{2,1,0:T(8,128)(2,1)}, bf16[4,192,768]{2,1,0:T(8,128)(2,1)}, bf16[4,192,768]{2,1,0:T(8,1...) custom-call(bf16[4,4,192,768]{3,2,1,0:T(8,128)(2,1)} %pad_maximum_fusion.refs_0_, ...), custom_call_target="tpu_custom_call" | custom-call | tf_op jit(solution)/shard_map/reduce_grads/pallas_call | solution.py:553
  793.3 2.9 copy.53
  801.3 3.8 maximum_convert_fusion
  (746 shorter events, 305.5 us)
Async XLA Ops:
  7.2 156.8 %all-gather.5.cloned.1.call-start = ((), (), s32[]{:S(2)}) async-start(), calls=%async_computation.4 | async-start | bytes 1966080 | tf_op jit(solution)/shard_map/all_gather | solution.py:680
  129.2 7.4 copy-start.36
  135.6 85.6 %copy-start.6 = (bf16[1,4,192,768]{3,2,1,0:T(8,128)(2,1)}, bf16[1,4,192,768]{3,2,1,0:T(8,128)(2,1)S(1)}, u32[]{:S(2)}) copy-start(bf16[1,4,192,768]{3,2,1,0:T(8,128)(2,1)S(1)} %get-tuple-element.610) | copy-start | bytes 3538948
  135.6 89.0 %copy-start.8 = (bf16[1,4,192,768]{3,2,1,0:T(8,128)(2,1)}, bf16[1,4,192,768]{3,2,1,0:T(8,128)(2,1)S(1)}, u32[]{:S(2)}) copy-start(bf16[1,4,192,768]{3,2,1,0:T(8,128)(2,1)S(1)} %get-tuple-element.577) | copy-start | bytes 3538948
  138.0 48.0 %all-gather.7.cloned.1.call-start = ((), (), s32[]{:S(2)}) async-start(), calls=%async_computation.5 | async-start | bytes 1966080 | tf_op jit(solution)/shard_map/all_gather | solution.py:679
  140.6 117.2 %all-gather.11.cloned.1.call-start = ((), (), s32[]{:S(2)}) async-start(), calls=%async_computation.7 | async-start | bytes 1966080 | tf_op jit(solution)/shard_map/all_gather | solution.py:679
  143.3 92.8 %copy-start.88 = (f32[768]{0:T(1024)}, f32[768]{0:T(1024)S(1)}, u32[]{:S(2)}) copy-start(f32[768]{0:T(1024)S(1)} %add.321) | copy-start | bytes 9220
  186.0 35.2 %copy-start.37 = (bf16[1,256,768]{2,1,0:T(8,128)(2,1)S(1)}, bf16[1,256,768]{2,1,0:T(8,128)(2,1)}, u32[]{:S(2)}) copy-start(bf16[1,256,768]{2,1,0:T(8,128)(2,1)} %param.20) | copy-start | bytes 1179652
  222.9 10.9 %copy-start.91 = (f32[256]{0:T(256)}, f32[256]{0:T(256)S(1)}, u32[]{:S(2)}) copy-start(f32[256]{0:T(256)S(1)} %broadcast_multiply_fusion.3) | copy-start | bytes 3076
  223.2 10.6 %copy-start.96 = (f32[256]{0:T(256)}, f32[256]{0:T(256)S(1)}, u32[]{:S(2)}) copy-start(f32[256]{0:T(256)S(1)} %fusion.96) | copy-start | bytes 3076
  225.2 8.6 %copy-start.66 = (f32[256,768]{1,0:T(8,128)}, f32[256,768]{1,0:T(8,128)S(1)}, u32[]{:S(2)}) copy-start(f32[256,768]{1,0:T(8,128)S(1)} %fusion.118) | copy-start | bytes 2359300
  225.5 8.3 %slice-start = ((s8[4718592]{0:T(1024)(128)(4,1)}), s8[4194304]{0:T(1024)(128)(4,1)S(1)}, s32[]{:S(2)}) async-start(s8[4718592]{0:T(1024)(128)(4,1)} %bitcast.527), calls=%async_computation.12 | async-start | bytes 8388608
  225.9 7.8 copy-start.68
  226.0 7.8 copy-start.125
  226.0 7.8 slice-start.1
  236.7 12.0 %copy-start.39 = (bf16[256,768]{1,0:T(8,128)(2,1)}, bf16[256,768]{1,0:T(8,128)(2,1)S(1)}, u32[]{:S(2)}) copy-start(bf16[256,768]{1,0:T(8,128)(2,1)S(1)} %fusion.59) | copy-start | bytes 1179652
  238.0 41.5 %all-gather.9.cloned.1.call-start = ((), (), s32[]{:S(2)}) async-start(), calls=%async_computation.6 | async-start | bytes 1966080 | tf_op jit(solution)/shard_map/all_gather | solution.py:680
  241.3 196.2 %reduce-scatter.5.cloned.1.call-start = ((), (), s32[]{:S(2)}) async-start(), calls=%async_computation.8 | async-start | bytes 1966080 | tf_op jit(solution)/shard_map/reduce_scatter | solution.py:755
  333.3 8.2 slice-start.2
  409.2 59.1 %reduce-scatter.7.cloned.1.call-start = ((), (), s32[]{:S(2)}) async-start(), calls=%async_computation.9 | async-start | bytes 1966080 | tf_op jit(solution)/shard_map/reduce_scatter | solution.py:758
  409.8 177.0 %reduce-scatter.11.cloned.1.call-start = ((), (), s32[]{:S(2)}) async-start(), calls=%async_computation.11 | async-start | bytes 1966080 | tf_op jit(solution)/shard_map/reduce_scatter | solution.py:758
  415.8 21.7 %copy-start.15 = (bf16[1,4,192,768]{3,2,1,0:T(8,128)(2,1)S(1)}, bf16[1,4,192,768]{3,2,1,0:T(8,128)(2,1)}, u32[]{:S(2)}) copy-start(bf16[1,4,192,768]{3,2,1,0:T(8,128)(2,1)} %get-tuple-element.605) | copy-start | bytes 3538948
  421.2 47.1 %copy-start.95 = (f32[256]{0:T(256)S(1)}, f32[256]{0:T(256)}, u32[]{:S(2)}) copy-start(f32[256]{0:T(256)} %copy-done.93) | copy-start | bytes 3076
  440.2 31.2 %copy-start.120 = (f32[256]{0:T(256)S(1)}, f32[256]{0:T(256)}, u32[]{:S(2)}) copy-start(f32[256]{0:T(256)} %copy-done.119) | copy-start | bytes 3076
  488.8 59.2 %copy-start.35 = (bf16[6,256,128]{1,2,0:T(8,128)(2,1)S(1)}, bf16[6,256,128]{1,2,0:T(8,128)(2,1)}, u32[]{:S(2)}) copy-start(bf16[6,256,128]{1,2,0:T(8,128)(2,1)} %copy-done.33) | copy-start | bytes 1179652
  488.8 59.2 %copy-start.77 = (bf16[768,256]{1,0:T(8,128)(2,1)S(1)}, bf16[768,256]{1,0:T(8,128)(2,1)}, u32[]{:S(2)}) copy-start(bf16[768,256]{1,0:T(8,128)(2,1)} %copy.44) | copy-start | bytes 1179652
  547.7 59.8 %reduce-scatter.9.cloned.1.call-start = ((), (), s32[]{:S(2)}) async-start(), calls=%async_computation.10 | async-start | bytes 1966080 | tf_op jit(solution)/shard_map/reduce_scatter | solution.py:755
  556.7 8.2 %copy-start.98 = (f32[768]{0:T(1024)S(1)}, f32[768]{0:T(1024)}, u32[]{:S(2)}) copy-start(f32[768]{0:T(1024)} %get-tuple-element.432) | copy-start | bytes 9220
  556.7 8.8 %copy-start.55 = (bf16[256,768]{0,1:T(8,128)(2,1)S(1)}, bf16[256,768]{0,1:T(8,128)(2,1)}, u32[]{:S(2)}) copy-start(bf16[256,768]{0,1:T(8,128)(2,1)} %reduce-scatter.7.cloned.1.call-done) | copy-start | bytes 1179652
  556.7 9.0 %copy-start.30 = (bf16[256,3072]{1,0:T(8,128)(2,1)S(1)}, bf16[256,3072]{1,0:T(8,128)(2,1)}, u32[]{:S(2)}) copy-start(bf16[256,3072]{1,0:T(8,128)(2,1)} %copy-done.29) | copy-start | bytes 4718596
  586.7 22.4 %copy-start.50 = (bf16[1,4,192,768]{3,2,1,0:T(8,128)(2,1)S(1)}, bf16[1,4,192,768]{3,2,1,0:T(8,128)(2,1)}, u32[]{:S(2)}) copy-start(bf16[1,4,192,768]{3,2,1,0:T(8,128)(2,1)} %fusion.34) | copy-start | bytes 3538948
  793.3 8.0 copy-start.79
  (106 other events, 259.6 us)
Sparse Core Ops, SparseCore 0:
  138.1 25.8 all-gather.4
  166.1 19.8 all-gather.6
  238.1 19.6 all-gather.10
  259.8 19.6 all-gather.8
  409.3 28.1 reduce-scatter.4
  440.1 28.1 reduce-scatter.6
  547.8 28.1 reduce-scatter.10
  579.3 28.1 reduce-scatter.8
